TPU v7x, 256 devices: a whole 4x4x8 slice. The times are simulated.
256 devices in a mesh: gz: 4 (over x), row: 4 (over y), col: 16 (over z, core).
Axes of the slice: x: 4, y: 4, z: 8, core: 2. Of those that a mesh axis runs over, the one named last changes fastest.
Arguments:
- leaf_rhs: float32 [512, 256, 512], P(('gz', 'col')), may hold values from -6 to 6
- leaf_inv: bfloat16 [512, 512, 512], P(('gz', 'col'), 'row'), as said below
- leaf_lower_mid: bfloat16 [512, 512, 512], P(('gz', 'col'), None, 'row'), may hold values from -0.09375 to 0.09375
- leaf_lower_coupling: bfloat16 [512, 3, 512, 512], P(('gz', 'col'), None, None, 'row'), may hold values from -0.015625 to 0.015625
- leaf_parent: int32 [512], P(('gz', 'col')), may hold values from 0 to 15
- leaf_pattern: int32 [512, 3], P(('gz', 'col')), may hold values 0 or 1
- mid_rhs: float32 [64, 256, 512], P(('gz', 'col')), may hold values from -6 to 6
- parent_diagonal_inverse: bfloat16 [64, 512, 512], P(('gz', 'col'), 'row'), as said below
- mid_lower: bfloat16 [64, 3, 512, 512], P(('gz', 'col'), None, None, 'row'), may hold values from -0.046875 to 0.046875
- mid_pattern: int32 [64, 2], P(('gz', 'col')), may hold values 0 or 1
- top_rhs: float32 [4, 256, 512], P('gz'), may hold values from -6 to 6
- top_inv: bfloat16 [4, 512, 512], P('gz', 'row'), as said below
- top_lower: bfloat16 [4, 2, 512, 512], P('gz', None, None, 'row'), may hold values from -0.1875 to 0.1875
- apex_rhs: float32 [3, 256, 512], replicated, may hold values from -6 to 6
- apex_inv: bfloat16 [3, 512, 512], P(None, 'row'), as said below
- apex_lower: bfloat16 [2, 512, 512], P(None, None, 'row'), may hold values from -0.25 to 0.25
Outputs:
- leaf_solution: float32 [512, 256, 512], P(('gz', 'col'), None, 'row')
- mid_solution: float32 [64, 256, 512], P(('gz', 'col'), None, 'row')
- top_solution: float32 [4, 256, 512], P('gz', None, 'row')
- apex_solution: float32 [3, 256, 512], P(None, 'gz', 'row')
Inputs may be any that keep to these rules, and one draw needn't show every extreme that they name: `leaf_inv`: each diagonal-block inverse is lower triangular with a unit diagonal. `parent_diagonal_inverse`: lower triangular with a unit diagonal. `top_inv`: lower triangular with a unit diagonal. `apex_inv`: lower triangular with a unit diagonal.
All inputs are finite; a program needn't handle non-finite values. No bound on the sum of `leaf_pattern` or of `mid_pattern` on one device may be relied on, other than what follows from the above.
Results may differ from a plain program's by a relative error of at most 0.015.
Values may be sent and summed in bfloat16 or wider, within the bound.
A program may use at most 128 MiB of HBM per device.

v0:
```python
import jax
import jax.numpy as jnp
from jax import lax
from jax.sharding import PartitionSpec as P


def from_partner(block, axis, apart):
    count = lax.axis_size(axis)
    route = []
    for low in range(count):
        high = low | 1 << apart
        if high != low and high < count:
            route += [(low, high), (high, low)]
    return lax.ppermute(block, axis, route)


def per_device(
    leaf_rhs,
    leaf_inv,
    leaf_lower_mid,
    leaf_lower_coupling,
    leaf_parent,
    leaf_pattern,
    mid_rhs,
    parent_diagonal_inverse,
    mid_lower,
    mid_pattern,
    top_rhs,
    top_inv,
    top_lower,
    apex_rhs,
    apex_inv,
    apex_lower,
):
    col_count = lax.axis_size("col")
    leaf_solved = jnp.einsum(
        "lrb,lcb->lrc", leaf_rhs.astype(jnp.bfloat16), leaf_inv, preferred_element_type=jnp.float32
    )
    leaf_round = leaf_solved.astype(jnp.bfloat16)
    toward_parent = jnp.einsum(
        "lrc,lac->lra", leaf_round, leaf_lower_mid, preferred_element_type=jnp.float32
    )
    to_up = jnp.einsum(
        "lrc,lkac->lkra", leaf_round, leaf_lower_coupling, preferred_element_type=jnp.float32
    )
    up_weight = leaf_pattern.astype(jnp.float32)
    layer_up = jnp.einsum("lk,lkra->kra", up_weight, to_up, precision=lax.Precision.HIGHEST)
    parent_ids = lax.broadcasted_iota(jnp.int32, (leaf_parent.shape[0], col_count), 1)
    onehot = (leaf_parent[:, None] == parent_ids).astype(jnp.float32)
    mid_terms = jnp.einsum("lm,lra->mra", onehot, toward_parent, precision=lax.Precision.HIGHEST)
    summed = lax.psum_scatter(mid_terms, "col", scatter_dimension=0, tiled=True)
    summed = lax.psum(summed, "row")
    parent_prepared = (mid_rhs - summed).astype(jnp.bfloat16)
    parent_unknowns = jnp.einsum(
        "atg,adg->atd", parent_prepared, parent_diagonal_inverse, preferred_element_type=jnp.float32
    )
    mid_round = parent_unknowns.astype(jnp.bfloat16)
    mid_up = jnp.einsum(
        "rc,kac->kra", mid_round[0], mid_lower[0], preferred_element_type=jnp.float32
    )
    mid_weight = jnp.concatenate([jnp.ones((1,), jnp.float32), mid_pattern[0].astype(jnp.float32)])
    layer_part = layer_up + mid_weight[:, None, None] * mid_up
    layer_full = lax.psum(layer_part, ("row", "col"))
    top_ready = (top_rhs[0] - layer_full[0]).astype(jnp.bfloat16)
    top_solved = jnp.einsum("rb,cb->rc", top_ready, top_inv[0], preferred_element_type=jnp.float32)
    top_round = top_solved.astype(jnp.bfloat16)
    top_up = jnp.einsum("rc,kac->kra", top_round, top_lower[0], preferred_element_type=jnp.float32)
    first_row = (lax.axis_index("row") == 0).astype(jnp.float32)
    carried = top_up + first_row * layer_full[1:]
    pair_index = lax.axis_index("gz") // 2
    paired = carried + from_partner(carried.astype(jnp.bfloat16), "gz", 0).astype(carried.dtype)
    paired = lax.psum(paired, "row")
    front_rhs = lax.dynamic_index_in_dim(apex_rhs, pair_index, 0, keepdims=False)
    front_inv = lax.dynamic_index_in_dim(apex_inv, pair_index, 0, keepdims=False)
    front_lower = lax.dynamic_index_in_dim(apex_lower, pair_index, 0, keepdims=False)
    local_unknowns = jnp.einsum(
        "rb,cb->rc",
        (front_rhs - paired[0]).astype(jnp.bfloat16),
        front_inv,
        preferred_element_type=jnp.float32,
    )
    own_up = jnp.einsum(
        "rc,ac->ra",
        local_unknowns.astype(jnp.bfloat16),
        front_lower,
        preferred_element_type=jnp.float32,
    )
    pair_last = paired[1] + lax.psum(own_up.astype(jnp.bfloat16), "row").astype(jnp.float32)
    other_last, other_solved = (
        from_partner(pair_last.astype(jnp.bfloat16), "gz", 1).astype(pair_last.dtype),
        from_partner(local_unknowns.astype(jnp.bfloat16), "gz", 1).astype(local_unknowns.dtype),
    )
    last_sum = pair_last + other_last
    leading = pair_index == 0
    front_solved = jnp.stack(
        [
            jnp.where(leading, local_unknowns, other_solved),
            jnp.where(leading, other_solved, local_unknowns),
        ]
    )
    last_solved = jnp.einsum(
        "rb,cb->rc",
        (apex_rhs[2] - last_sum).astype(jnp.bfloat16),
        apex_inv[2],
        preferred_element_type=jnp.float32,
    )
    apex_unknowns = jnp.concatenate([front_solved, last_solved[None]], axis=0)
    quarter = apex_unknowns.shape[1] // lax.axis_size("gz")
    apex_part = lax.dynamic_slice_in_dim(apex_unknowns, lax.axis_index("gz") * quarter, quarter, 1)
    return (leaf_solved, parent_unknowns, top_solved[None], apex_part)


def solution(mesh):
    placed = (
        P(("gz", "col"), None, None),
        P(("gz", "col"), "row", None),
        P(("gz", "col"), None, "row"),
        P(("gz", "col"), None, None, "row"),
        P(("gz", "col")),
        P(("gz", "col"), None),
        P(("gz", "col"), None, None),
        P(("gz", "col"), "row", None),
        P(("gz", "col"), None, None, "row"),
        P(("gz", "col"), None),
        P("gz", None, None),
        P("gz", "row", None),
        P("gz", None, None, "row"),
        P(),
        P(None, "row", None),
        P(None, None, "row"),
    )
    return jax.shard_map(
        per_device,
        mesh=mesh,
        in_specs=placed,
        out_specs=(
            P(("gz", "col"), None, "row"),
            P(("gz", "col"), None, "row"),
            P("gz", None, "row"),
            P(None, "gz", "row"),
        ),
        check_vma=False,
    )
```

profile of v0, /device:TPU:1, one launch (start us, length us, event | category | flops | bytes accessed | tf_op | source)
XLA Modules:
  0.0 476.8 jit_solution(15525845745413372762)
XLA Ops:
  7.2 0.0 copy-start
  7.2 0.0 reduce-scatter.2.cloned.1.call-start
  7.2 0.0 copy-start.2
  7.2 3.3 fusion.4
  10.6 0.0 copy-start.1
  10.6 1.0 copy-done.1
  11.6 0.0 copy-done.2
  11.6 0.0 copy-start.8
  11.6 0.7 fusion.26
  12.3 0.0 copy-done.8
  12.3 5.8 %fusion.2 = f32[16,256,512]{2,0,1:T(8,128)S(1)} fusion(f32[8,256,512]{2,1,0:T(8,128)S(1)} %fusion.26, s32[8]{0:T(128)S(1)} %copy-done.8), kind=kOutput, calls=%fused_computation.3 | convolution fusion | flops 201326720 | bytes 12582944 | tf_op jit(solution)/shard_map/lm,lra->mra/dot_general | solution.py:50
  18.1 8.1 %copy.23 = f32[16,256,512]{2,1,0:T(8,128)} copy(f32[16,256,512]{2,0,1:T(8,128)S(1)} %fusion.2) | data formatting | bytes 16777216 | tf_op jit(solution)/shard_map/lm,lra->mra/dot_general | solution.py:50
  26.1 0.0 copy-start.9
  26.1 0.0 copy-start.7
  26.2 0.0 reduce-scatter.2.cloned.1.call-update
  26.2 0.0 all-reduce.5.cloned.1.call-start
  26.2 0.6 copy-done.9
  26.8 0.1 pad_maximum_fusion
  26.9 0.0 copy-done.7
  26.9 0.0 copy-done
  26.9 7.5 %convolution_bitcast_fusion = f32[8,3,256,512]{3,2,1,0:T(8,128)} fusion(bf16[8,3,512,128]{3,2,1,0:T(8,128)(2,1)S(1)} %copy-done, f32[8,256,128]{2,1,0:T(8,128)} %copy-done.1), kind=kOutput, calls=%fused_computation.2 | convolution fusion | flops 805568512 | bytes 16777216 | tf_op jit(solution)/shard_map/lrc,lkac->lkra/dot_general | solution.py:43
  34.4 63.3 %reduce-scatter.2.cloned.1.call-done = f32[1,256,512]{2,1,0:T(8,128)} async-done(((f32[16,256,512]{2,1,0:T(8,128)}), f32[1,256,512]{2,1,0:T(8,128)}) %reduce-scatter.2.cloned.1.call-update) | async-done | bytes 524304 | tf_op jit(solution)/shard_map/reduce_scatter | solution.py:51
  97.8 0.0 all-reduce.5.cloned.1.call-update
  97.8 0.0 copy-start.5
  97.8 0.2 all-reduce.7.cloned.1.call-start
  98.0 22.7 %fusion = f32[3,1,256,512]{3,1,2,0:T(1,128)} fusion(f32[8,3,256,512]{3,2,1,0:T(8,128)} %convolution_bitcast_fusion, f32[8,3,1,1]{0,1,2,3:T(4,128)S(1)} %convert_bitcast_fusion), kind=kOutput, calls=%fused_computation | convolution fusion | flops 37748736 | bytes 14155872 | tf_op jit(solution)/shard_map/lk,lkra->kra/dot_general | solution.py:47
  120.7 0.0 copy-start.6
  120.7 27.4 %all-reduce.5.cloned.1.call-done = f32[1,256,512]{2,1,0:T(8,128)} async-done(((f32[1,256,512]{2,1,0:T(8,128)}), f32[1,256,512]{2,1,0:T(8,128)}) %all-reduce.5.cloned.1.call-update) | async-done | bytes 524304 | tf_op jit(solution)/shard_map/psum | solution.py:52
  148.2 0.0 copy-done.5
  148.2 1.4 fusion.15
  149.6 0.0 copy-start.3
  149.6 3.1 bitcast_add_fusion
  152.8 0.0 all-reduce.7.cloned.1.call-update
  152.8 0.0 all-reduce.9.cloned.1.call-start
  152.8 188.6 %all-reduce.7.cloned.1.call-done = f32[3,256,512]{2,1,0:T(8,128)} async-done(((f32[3,256,512]{2,1,0:T(8,128)}), f32[3,256,512]{2,1,0:T(8,128)}) %all-reduce.7.cloned.1.call-update) | async-done | bytes 1572880 | tf_op jit(solution)/shard_map/psum | solution.py:63
  341.4 0.0 copy-done.6
  341.4 1.4 fusion.19
  342.9 0.0 copy-done.3
  342.9 0.0 copy-start.4
  342.9 1.6 fusion.50
  344.6 1.3 collective-permute-start
  345.8 10.0 %collective-permute-done = bf16[2,256,512]{2,1,0:T(8,128)(2,1)S(1)} collective-permute-done((bf16[2,256,512]{2,1,0:T(8,128)(2,1)S(1)}, bf16[2,256,512]{2,1,0:T(8,128)(2,1)S(1)}, u32[]{:S(2)}, u32[]{:S(2)}) %collective-permute-start) | collective-permute-done | bytes 524320 | tf_op jit(solution)/shard_map/ppermute | solution.py:14
  355.8 1.2 convert_add_fusion
  357.0 0.0 all-reduce.9.cloned.1.call-update
  357.0 0.0 copy-done.4
  357.0 0.0 all-reduce.11.cloned.1.call-start
  357.1 51.0 %all-reduce.9.cloned.1.call-done = f32[2,256,512]{2,1,0:T(8,128)} async-done(((f32[2,256,512]{2,1,0:T(8,128)}), f32[2,256,512]{2,1,0:T(8,128)}) %all-reduce.9.cloned.1.call-update) | async-done | bytes 1048592 | tf_op jit(solution)/shard_map/psum | solution.py:72
  408.1 2.1 fusion.51
  410.2 1.9 convolution_convert_fusion
  412.0 0.0 all-reduce.11.cloned.1.call-update
  412.1 2.8 collective-permute-start.1
  414.9 44.3 %all-reduce.11.cloned.1.call-done = bf16[256,512]{1,0:T(8,128)(2,1)} async-done(((bf16[256,512]{1,0:T(8,128)(2,1)}), bf16[256,512]{1,0:T(8,128)(2,1)}) %all-reduce.11.cloned.1.call-update) | async-done | bytes 262160 | tf_op jit(solution)/shard_map/psum | solution.py:88
  459.2 1.9 fusion.13
  461.1 2.7 collective-permute-start.2
  463.8 0.0 collective-permute-done.1
  463.8 0.9 fusion.29
  464.6 3.4 collective-permute-done.2
  468.0 1.5 convolution_bitcast_fusion.2
  469.6 0.7 fusion.39
  (2 shorter events, 0.0 us)
Async XLA Ops:
  7.2 19.7 %copy-start = (bf16[8,3,512,128]{3,2,1,0:T(8,128)(2,1)S(1)}, bf16[8,3,512,128]{3,2,1,0:T(8,128)(2,1)}, u32[]{:S(2)}) copy-start(bf16[8,3,512,128]{3,2,1,0:T(8,128)(2,1)} %param.19) | copy-start | bytes 9437188
  7.2 90.6 %reduce-scatter.2.cloned.1.call-start = ((), (), s32[]{:S(2)}) async-start(), calls=%async_computation.1 | async-start | bytes 8912896 | tf_op jit(solution)/shard_map/reduce_scatter | solution.py:51
  7.2 4.3 copy-start.2
  10.6 1.0 copy-start.1
  11.6 0.7 copy-start.8
  26.1 0.7 copy-start.9
  26.1 0.7 copy-start.7
  26.2 122.0 %all-reduce.5.cloned.1.call-start = ((), (), s32[]{:S(2)}) async-start(), calls=%async_computation.2 | async-start | bytes 1048576 | tf_op jit(solution)/shard_map/psum | solution.py:52
  97.8 50.4 %copy-start.5 = (bf16[1,128,512]{2,1,0:T(8,128)(2,1)S(1)}, bf16[1,128,512]{2,1,0:T(8,128)(2,1)}, u32[]{:S(2)}) copy-start(bf16[1,128,512]{2,1,0:T(8,128)(2,1)} %param.23) | copy-start | bytes 393220
  97.8 243.6 %all-reduce.7.cloned.1.call-start = ((), (), s32[]{:S(2)}) async-start(), calls=%async_computation.3 | async-start | bytes 3145728 | tf_op jit(solution)/shard_map/psum | solution.py:63
  120.7 220.7 %copy-start.6 = (bf16[1,128,512]{2,1,0:T(8,128)(2,1)S(1)}, bf16[1,128,512]{2,1,0:T(8,128)(2,1)}, u32[]{:S(2)}) copy-start(bf16[1,128,512]{2,1,0:T(8,128)(2,1)} %param.27) | copy-start | bytes 393220
  149.6 193.3 %copy-start.3 = (f32[256,128]{1,0:T(8,128)}, f32[256,128]{1,0:T(8,128)S(1)}, u32[]{:S(2)}) copy-start(f32[256,128]{1,0:T(8,128)S(1)} %fusion.15) | copy-start | bytes 393220
  152.8 255.3 %all-reduce.9.cloned.1.call-start = ((), (), s32[]{:S(2)}) async-start(), calls=%async_computation.4 | async-start | bytes 2097152 | tf_op jit(solution)/shard_map/psum | solution.py:72
  342.9 14.1 %copy-start.4 = (f32[256,128]{1,0:T(8,128)}, f32[256,128]{1,0:T(8,128)S(1)}, u32[]{:S(2)}) copy-start(f32[256,128]{1,0:T(8,128)S(1)} %fusion.19) | copy-start | bytes 393220
  344.6 11.2 %collective-permute-start = (bf16[2,256,512]{2,1,0:T(8,128)(2,1)S(1)}, bf16[2,256,512]{2,1,0:T(8,128)(2,1)S(1)}, u32[]{:S(2)}, u32[]{:S(2)}) collective-permute-start(bf16[2,256,512]{2,1,0:T(8,128)(2,1)S(1)} %get-tuple-element.6), channel_id=1, source_target_pairs={{0,64},{64,0},{128,192},{192,128},{1,65},{65,1},{129,193},{193,129... | collective-permute-start | bytes 1572872 | tf_op jit(solution)/shard_map/ppermute | solution.py:14
  357.0 102.2 %all-reduce.11.cloned.1.call-start = ((), (), s32[]{:S(2)}) async-start(), calls=%async_computation.5 | async-start | bytes 524288 | tf_op jit(solution)/shard_map/psum | solution.py:88
  412.1 51.7 %collective-permute-start.1 = (bf16[256,128]{1,0:T(8,128)(2,1)}, bf16[256,128]{1,0:T(8,128)(2,1)}, u32[]{:S(2)}, u32[]{:S(2)}) collective-permute-start(bf16[256,128]{1,0:T(8,128)(2,1)} %get-tuple-element.8), channel_id=1, source_target_pairs={{0,128},{128,0},{64,192},{192,64},{1,129},{129,1},{65,193},{193,65... | collective-permute-start | bytes 196616 | tf_op jit(solution)/shard_map/ppermute | solution.py:14
  461.1 6.9 %collective-permute-start.2 = (bf16[256,512]{1,0:T(8,128)(2,1)}, bf16[256,512]{1,0:T(8,128)(2,1)S(1)}, u32[]{:S(2)}, u32[]{:S(2)}) collective-permute-start(bf16[256,512]{1,0:T(8,128)(2,1)} %fusion.13), channel_id=1, source_target_pairs={{0,128},{128,0},{64,192},{192,64},{1,129},{129,1},{65,193},{193,65... | collective-permute-start | bytes 786440 | tf_op jit(solution)/shard_map/ppermute | solution.py:14
Sparse Core Ops, SparseCore 0:
  26.3 71.4 reduce-scatter.1
  100.1 48.0 all-reduce.4
  152.9 188.4 all-reduce.6
  357.1 50.9 all-reduce.8
  412.2 46.9 all-reduce.10
where the time goes:
time: 480 us; the launch traced here: 477 us
  waiting for transfers between devices  388 us (81%)
  matrix products  53.2 us (11%)
  between operations  14 us (3%)
  local copies, waits for them, and re-layouts  9.66 us (2%)
  starting transfers between devices  7.14 us (1%)
    psum x1, waiting for transfers between devices, per_device(): layer_full = lax.psum(layer_part, ('row', 'col'))  189 us
    reduce_scatter x1, waiting for transfers between devices, per_device(): summed = lax.psum_scatter(mid_terms, 'col', scatter_dimension=0, tiled=True)  63.3 us
    psum x1, waiting for transfers between devices, per_device(): paired = lax.psum(paired, 'row')  51 us
    psum x1, waiting for transfers between devices, per_device(): lax.psum(own_up.astype(jnp.bfloat16), 'row').astype(jnp.float32)  44.3 us
    psum x1, waiting for transfers between devices, per_device(): summed = lax.psum(summed, 'row')  27.4 us
    dot_general x1, matrix products, per_device(): jnp.einsum('lk,lkra->kra', up_weight, to_up, precision=lax.Precision.HIGH...  22.7 us
    ppermute x3, waiting for transfers between devices, from_partner(): return lax.ppermute(block, axis, route)  13.3 us
  transfers between devices with their start and end apart: 8, of which 7 were waited for; matrix products, arithmetic and copies ran while one was open for 7% of the time, Pallas kernels for 0%

commit v1 on v0

v1 whole, which is shorter than its diff:
```python
import jax
import jax.numpy as jnp
from jax import lax
from jax.experimental import pallas as pl
from jax.experimental.pallas import tpu as pltpu
from jax.sharding import PartitionSpec as P

MESH = pl.DeviceIdType.MESH
F32 = jnp.float32
BF16 = jnp.bfloat16
N_LEAF = 8
SLICE = 128
HALF = 128
SHARE = 16


def dot_nt(a, b):
    return lax.dot_general(a, b, (((1,), (1,)), ((), ())), preferred_element_type=F32)


def send(src, dst, send_sem, recv_sem, where):
    return pltpu.make_async_remote_copy(
        src_ref=src,
        dst_ref=dst,
        send_sem=send_sem,
        recv_sem=recv_sem,
        device_id=where,
        device_id_type=MESH,
    )


def kernel(
    parent_s,
    pattern_s,
    midpat_s,
    rhs_h,
    inv_h,
    lm_h,
    lc_h,
    midrhs_h,
    pinv_h,
    midl_h,
    toprhs_h,
    topinv_h,
    topl_h,
    apexrhs_h,
    apexinv_h,
    apexl_h,
    leaf_o,
    mid_o,
    top_o,
    apex_o,
    rhs_v,
    inv_v,
    lm_v,
    lc_v,
    midrhs_v,
    pinv_v,
    midl_v,
    toprhs_v,
    topinv_v,
    topl_v,
    apexrhs_v,
    apexinv_v,
    apexl_v,
    sol_v,
    rnd_v,
    masked_v,
    up_v,
    yopp_v,
    yfwd_v,
    ybwd_v,
    yown_v,
    y1_v,
    ysend_v,
    y2_v,
    part_v,
    sib_v,
    pid_v,
    pidsib_v,
    acc_v,
    zsend_v,
    zrecv_v,
    mt_v,
    msol_v,
    csend_v,
    crecv_v,
    ownp_v,
    zsc_v,
    zin_v,
    rsend_v,
    rrecv_v,
    tops_v,
    q1_v,
    q1r_v,
    e_v,
    er_v,
    u_v,
    ur_v,
    fsend_v,
    fother_v,
    fins_v,
    fin_v,
    ld_leaf,
    ld_misc,
    out_leaf,
    out_misc,
    y1_ss,
    y1_rs,
    y2_ss,
    y2_rs,
    sib_ss,
    sib_rs,
    pid_sem,
    z_ss,
    z_rs,
    mt_ss,
    mt_rs,
    c_ss,
    c_rs,
    zin_ss,
    zin_rs,
    x_ss,
    x_rs,
):
    g = lax.axis_index("gz")
    r = lax.axis_index("row")
    c = lax.axis_index("col")
    z, core = c // 2, c % 2
    pair = g // 2
    block = core * 128 + z * SHARE
    sibling = {"col": 2 * z + (1 - core)}

    def rows(start, count, unit):
        return pl.ds(pl.multiple_of(start, unit), count)

    barrier = pltpu.get_barrier_semaphore()

    def greet(where):
        pl.semaphore_signal(barrier, inc=1, device_id=where, device_id_type=MESH)

    for apart in range(1, 16):
        greet({"col": (c + apart) % 16})
    for apart in range(1, 16):
        greet({"gz": (g + apart // 4) % 4, "row": (r + apart % 4) % 4})
    for i in range(4):
        giver = 2 * ((g % 2) * 4 + i) + g // 2
        greet({"gz": (g + 1 + ((c - giver + 16) % 16) // 4) % 4, "col": giver})

    def leaf_loads(l):
        return (
            pltpu.make_async_copy(rhs_h.at[l], rhs_v.at[l], ld_leaf.at[l, 0]),
            pltpu.make_async_copy(inv_h.at[l], inv_v.at[l], ld_leaf.at[l, 1]),
            pltpu.make_async_copy(lm_h.at[l], lm_v.at[l], ld_leaf.at[l, 2]),
        )

    def coupling_load(l):
        return pltpu.make_async_copy(
            lc_h.at[l], lc_v.at[:, :, rows(l * SLICE, SLICE, SLICE)], ld_leaf.at[l, 3]
        )

    misc = (
        (midrhs_h.at[0, :, rows(r * SLICE, SLICE, SLICE)], midrhs_v),
        (pinv_h.at[0], pinv_v),
        (midl_h.at[0], midl_v),
        (toprhs_h.at[0, rows(block, SHARE, SHARE), :], toprhs_v),
        (topinv_h.at[0], topinv_v),
        (topl_h.at[0], topl_v),
        (apexrhs_h.at[pair, rows(block, SHARE, SHARE), :], apexrhs_v.at[0]),
        (apexrhs_h.at[2, rows(block, SHARE, SHARE), :], apexrhs_v.at[1]),
        (apexinv_h.at[pair], apexinv_v.at[0]),
        (apexinv_h.at[2], apexinv_v.at[1]),
        (apexl_h.at[pair], apexl_v),
    )
    misc = [pltpu.make_async_copy(s, d, ld_misc.at[i]) for i, (s, d) in enumerate(misc)]

    @pl.loop(0, N_LEAF)
    def _(l):
        for copy in leaf_loads(l):
            copy.start()

    @pl.loop(0, N_LEAF)
    def _(l):
        coupling_load(l).start()

    for copy in misc:
        copy.start()

    @pl.loop(0, N_LEAF)
    def _(l):
        pid_v[l] = jnp.full((8, 128), parent_s[l].astype(F32), F32)

    pl.semaphore_wait(barrier, 34)

    pid_copy = send(pid_v, pidsib_v, pid_sem.at[0], pid_sem.at[1], sibling)
    pid_copy.start()

    ahead, behind, across = (r + 1) % 4, (r + 3) % 4, (r + 2) % 4

    def y1_copies(l):
        return (
            send(
                yopp_v.at[l, pl.ds(0, HALF)], y1_v.at[l, 0], y1_ss.at[l, 0], y1_rs.at[l, 0],
                {"row": ahead},
            ),
            send(
                yopp_v.at[l, pl.ds(HALF, HALF)], y1_v.at[l, 1], y1_ss.at[l, 1], y1_rs.at[l, 1],
                {"row": behind},
            ),
        )

    def y2_copies(l):
        return (
            send(ysend_v.at[l, 0], y2_v.at[l, 0], y2_ss.at[l, 0], y2_rs.at[l, 0], {"row": ahead}),
            send(ysend_v.at[l, 1], y2_v.at[l, 1], y2_ss.at[l, 1], y2_rs.at[l, 1], {"row": behind}),
        )

    def sib_copy(l):
        return send(part_v.at[l], sib_v.at[l], sib_ss.at[l], sib_rs.at[l], sibling)

    def leaf_out(l):
        return pltpu.make_async_copy(sol_v.at[l], leaf_o.at[l], out_leaf.at[l])

    @pl.loop(0, N_LEAF)
    def _(l):
        load_rhs, load_inv, load_lm = leaf_loads(l)
        load_rhs.wait()
        load_inv.wait()
        solved = dot_nt(rhs_v[l].astype(BF16), inv_v[l])
        sol_v[l] = solved
        rounded = solved.astype(BF16)
        rnd_v[l] = rounded
        load_lm.wait()
        yopp_v[l] = dot_nt(rounded, lm_v[l, rows(across * SLICE, SLICE, SLICE), :]).astype(BF16)
        for copy in y1_copies(l):
            copy.start()
        leaf_out(l).start()
        yfwd_v[l] = dot_nt(rounded, lm_v[l, rows(ahead * SLICE, SLICE, SLICE), :])
        ybwd_v[l] = dot_nt(rounded, lm_v[l, rows(behind * SLICE, SLICE, SLICE), :])
        yown_v[l] = dot_nt(rounded, lm_v[l, rows(r * SLICE, SLICE, SLICE), :])

    @pl.loop(0, N_LEAF)
    def _(l):
        forward, backward = y1_copies(l)
        to_ahead, to_behind = y2_copies(l)
        forward.wait_recv()
        ysend_v[l, 0, :HALF] = (yfwd_v[l, :HALF] + y1_v[l, 0].astype(F32)).astype(BF16)
        ysend_v[l, 0, HALF:] = yfwd_v[l, HALF:].astype(BF16)
        to_ahead.start()
        backward.wait_recv()
        ysend_v[l, 1, :HALF] = ybwd_v[l, :HALF].astype(BF16)
        ysend_v[l, 1, HALF:] = (ybwd_v[l, HALF:] + y1_v[l, 1].astype(F32)).astype(BF16)
        to_behind.start()

    @pl.loop(0, N_LEAF)
    def _(l):
        coupling_load(l).wait()
        rounded = rnd_v[l].astype(F32)
        for k in range(3):
            weight = pattern_s[l, k].astype(F32)
            masked_v[k, :, rows(l * SLICE, SLICE, SLICE)] = (rounded * weight).astype(BF16)

    for k in range(3):
        up_v[k] = dot_nt(masked_v[k], lc_v[k])

    acc_v[...] = jnp.zeros_like(acc_v)

    def gather_parents(pids, terms):
        for t in range(8):
            wanted = (2 * t + core).astype(F32)
            hit = jnp.maximum(1.0 - jnp.abs(pids - wanted), 0.0)
            acc_v[t] += (terms.reshape(32, 8, 128) * hit[None]).reshape(256, 128)

    pid_copy.wait_recv()

    @pl.loop(0, N_LEAF)
    def _(l):
        for copy in y2_copies(l):
            copy.wait_recv()
        total = yown_v[l] + y2_v[l, 0].astype(F32) + y2_v[l, 1].astype(F32)
        part_v[l] = total.astype(BF16)
        sib_copy(l).start()
        gather_parents(pid_v[l], total)

        @pl.when(l > 0)
        def _():
            sib_copy(l - 1).wait_recv()
            gather_parents(pidsib_v[l - 1], sib_v[l - 1].astype(F32))

    sib_copy(N_LEAF - 1).wait_recv()
    gather_parents(pidsib_v[N_LEAF - 1], sib_v[N_LEAF - 1].astype(F32))

    def z_copy(way, dist, h):
        step = 1 if way == 0 else 7
        return send(
            zsend_v.at[way, dist - 1, h],
            zrecv_v.at[way, dist - 1, h],
            z_ss.at[way, dist - 1, h],
            z_rs.at[way, dist - 1, h],
            {"col": 2 * ((z + step) % 8) + core},
        )

    z_flows = []
    for dist in (4, 3, 2, 1):
        for late in (0, 1):
            for way in (0, 1):
                h = way if late else 1 - way
                if dist == 4 and not late:
                    continue
                z_flows.append((way, dist, h))
    for way, dist, h in z_flows:
        target = (z + dist) % 8 if way == 0 else (z + 8 - dist) % 8
        term = acc_v[target, h * HALF : (h + 1) * HALF]
        if (way, dist + 1, h) in z_flows:
            z_copy(way, dist + 1, h).wait_recv()
            term = term + zrecv_v[way, dist, h].astype(F32)
        zsend_v[way, dist - 1, h] = term.astype(BF16)
        z_copy(way, dist, h).start()

    def mt_copy(h, apart):
        return send(
            mt_v.at[r, h], mt_v.at[r, h], mt_ss.at[h, apart - 1], mt_rs.at[h, apart - 1],
            {"row": (r + apart) % 4},
        )

    def mt_arrival(h, apart):
        source = (r + 4 - apart) % 4
        return send(
            mt_v.at[source, h], mt_v.at[source, h], mt_ss.at[h, apart - 1],
            mt_rs.at[h, apart - 1], {"row": source},
        )

    misc[0].wait()
    for h in (0, 1):
        z_copy(0, 1, h).wait_recv()
        z_copy(1, 1, h).wait_recv()
        total = (
            midrhs_v[h * HALF : (h + 1) * HALF]
            - acc_v[z, h * HALF : (h + 1) * HALF]
            - zrecv_v[0, 0, h].astype(F32)
            - zrecv_v[1, 0, h].astype(F32)
        )
        mt_v[r, h] = total.astype(BF16)
        for apart in (1, 3, 2):
            mt_copy(h, apart).start()

    misc[1].wait()
    misc[2].wait()
    for h in (0, 1):
        for apart in (1, 2, 3):
            mt_arrival(h, apart).wait_recv()

    mid_weight = (None, midpat_s[0, 0].astype(F32), midpat_s[0, 1].astype(F32))

    def c_copy(k):
        return send(csend_v.at[k], crecv_v.at[k], c_ss.at[k], c_rs.at[k], sibling)

    def layer_half(h, store):
        right = jnp.concatenate([mt_v[i, h] for i in range(4)], axis=1)
        solved = dot_nt(right, pinv_v[...])
        msol_v[rows(h * HALF, HALF, HALF)] = solved
        rounded = solved.astype(BF16)
        for k in range(3):
            term = dot_nt(rounded, midl_v[k])
            if k:
                term = term * mid_weight[k]
            store(k, up_v[k, rows(h * HALF, HALF, HALF)] + term)

    def store_send(k, value):
        csend_v[k] = value.astype(BF16)
        c_copy(k).start()

    def store_own(k, value):
        ownp_v[k] = value

    layer_half(1 - core, store_send)
    layer_half(core, store_own)
    mid_out = pltpu.make_async_copy(msol_v, mid_o.at[0], out_misc.at[0])
    mid_out.start()

    def zin_copy(k, apart):
        target = (z + apart) % 8
        return send(
            zsc_v.at[k, rows(target * SHARE, SHARE, SHARE)], zin_v.at[k, apart - 1],
            zin_ss.at[k], zin_rs.at[k], {"col": 2 * target + core},
        )

    def all_of(buffer, send_sem, recv_sem):
        return send(buffer, buffer, send_sem, recv_sem, {"row": ahead})

    for k in range(3):
        c_copy(k).wait_recv()
        total = ownp_v[k] + crecv_v[k].astype(F32)
        ownp_v[k] = total
        zsc_v[k] = total.astype(BF16)
        for apart in (4, 3, 5, 2, 6, 1, 7):
            zin_copy(k, apart).start()

    def share_sum(k):
        all_of(zin_v.at[k], zin_ss.at[k], zin_rs.at[k]).wait_recv()
        total = ownp_v[k, rows(z * SHARE, SHARE, SHARE)]
        for i in range(7):
            total = total + zin_v[k, i].astype(F32)
        return total

    own = share_sum(0)
    rsend_v[...] = own.astype(BF16)
    for apart in (2, 1, 3):
        send(rsend_v, rrecv_v.at[apart - 1], x_ss.at[0], x_rs.at[0], {"row": (r + apart) % 4}).start()
    for i in range(3, 11):
        misc[i].wait()
    p1 = share_sum(1)
    p2 = share_sum(2)
    all_of(rrecv_v, x_ss.at[0], x_rs.at[0]).wait_recv()
    for i in range(3):
        own = own + rrecv_v[i].astype(F32)
    solved = dot_nt((toprhs_v[...] - own).astype(BF16), topinv_v[...])
    rounded = solved.astype(BF16)
    tops_v[rows(block, SHARE, SHARE)] = solved
    q1 = p1 + dot_nt(rounded, topl_v[0])
    q1_v[...] = q1.astype(BF16)
    mate = g + 1 - 2 * (g % 2)
    facing = 3 - g

    def to_group(src, dst, sem, other):
        for layer in (1, 0):
            for apart in (2, 1, 3, 0):
                if layer or apart:
                    send(
                        src, dst.at[4 * layer + apart - 1], x_ss.at[sem], x_rs.at[sem],
                        {"gz": other if layer else g, "row": (r + apart) % 4},
                    ).start()

    to_group(q1_v, q1r_v, 1, mate)
    e = p2 + dot_nt(rounded, topl_v[1])
    e_v[...] = e.astype(BF16)
    for apart in range(15, 0, -1):
        send(
            e_v, er_v.at[apart - 1], x_ss.at[2], x_rs.at[2],
            {"gz": (g + apart // 4) % 4, "row": (r + apart % 4) % 4},
        ).start()
    for apart in range(1, 16):
        mine = tops_v.at[rows(block, SHARE, SHARE)]
        send(mine, mine, x_ss.at[3], x_rs.at[3], {"col": (c + apart) % 16}).start()

    all_of(q1r_v, x_ss.at[1], x_rs.at[1]).wait_recv()
    for i in range(7):
        q1 = q1 + q1r_v[i].astype(F32)
    front = dot_nt((apexrhs_v[0] - q1).astype(BF16), apexinv_v[0])
    fsend_v[...] = front
    u = dot_nt(front.astype(BF16), apexl_v[...])
    u_v[...] = u.astype(BF16)
    to_group(u_v, ur_v, 4, facing)
    send(fsend_v, fother_v, x_ss.at[5], x_rs.at[5], {"gz": facing}).start()
    fins_v[pair] = front

    all_of(er_v, x_ss.at[2], x_rs.at[2]).wait_recv()
    for i in range(15):
        e = e + er_v[i].astype(F32)
    all_of(tops_v.at[pl.ds(0, 240)], x_ss.at[3], x_rs.at[3]).wait_recv()
    top_out = pltpu.make_async_copy(tops_v, top_o.at[0], out_misc.at[1])
    top_out.start()
    last = apexrhs_v[1] - e - u

    all_of(fother_v, x_ss.at[5], x_rs.at[5]).wait_recv()
    fins_v[1 - pair] = fother_v[...]
    all_of(ur_v, x_ss.at[4], x_rs.at[4]).wait_recv()
    for i in range(7):
        last = last - ur_v[i].astype(F32)
    fins_v[2] = dot_nt(last.astype(BF16), apexinv_v[1])

    holder = core * 2 + z // 4
    turn = (g - holder + 7) % 4
    for i in range(4):
        send(
            fins_v, fin_v.at[:, rows((z % 4) * SHARE, SHARE, SHARE)], x_ss.at[6], x_rs.at[6],
            {"gz": holder, "col": (c + 4 * turn + i) % 16},
        ).start()

    pid_copy.wait_send()

    @pl.loop(0, N_LEAF)
    def _(l):
        for copy in y1_copies(l) + y2_copies(l) + (sib_copy(l),):
            copy.wait_send()
        leaf_out(l).wait()

    for way, dist, h in z_flows:
        z_copy(way, dist, h).wait_send()
    for h in (0, 1):
        for apart in (1, 2, 3):
            mt_copy(h, apart).wait_send()
    for k in range(3):
        c_copy(k).wait_send()
        all_of(zin_v.at[k], zin_ss.at[k], zin_rs.at[k]).wait_send()
    all_of(rrecv_v, x_ss.at[0], x_rs.at[0]).wait_send()
    all_of(q1r_v, x_ss.at[1], x_rs.at[1]).wait_send()
    all_of(er_v, x_ss.at[2], x_rs.at[2]).wait_send()
    all_of(tops_v.at[pl.ds(0, 240)], x_ss.at[3], x_rs.at[3]).wait_send()
    all_of(ur_v, x_ss.at[4], x_rs.at[4]).wait_send()
    all_of(fother_v, x_ss.at[5], x_rs.at[5]).wait_send()
    all_of(fin_v, x_ss.at[6], x_rs.at[6]).wait()
    apex_out = pltpu.make_async_copy(fin_v, apex_o, out_misc.at[2])
    apex_out.start()
    mid_out.wait()
    top_out.wait()
    apex_out.wait()


def per_device(*args):
    (
        leaf_rhs, leaf_inv, leaf_lower_mid, leaf_lower_coupling, leaf_parent, leaf_pattern,
        mid_rhs, parent_diagonal_inverse, mid_lower, mid_pattern, top_rhs, top_inv, top_lower,
        apex_rhs, apex_inv, apex_lower,
    ) = args
    smem = pl.BlockSpec(memory_space=pltpu.SMEM)
    anywhere = pl.BlockSpec(memory_space=pl.ANY)
    V = pltpu.VMEM
    D = pltpu.SemaphoreType.DMA
    scratch = [
        V((8, 256, 512), F32),
        V((8, 128, 512), BF16),
        V((8, 512, 128), BF16),
        V((3, 512, 1024), BF16),
        V((256, 128), F32),
        V((128, 512), BF16),
        V((3, 512, 128), BF16),
        V((16, 512), F32),
        V((128, 512), BF16),
        V((2, 512, 128), BF16),
        V((2, 16, 512), F32),
        V((2, 128, 512), BF16),
        V((512, 128), BF16),
        V((8, 256, 128), F32),
        V((8, 256, 128), BF16),
        V((3, 256, 1024), BF16),
        V((3, 256, 512), F32),
        V((8, 256, 128), BF16),
        V((8, 256, 128), F32),
        V((8, 256, 128), F32),
        V((8, 256, 128), F32),
        V((8, 2, 128, 128), BF16),
        V((8, 2, 256, 128), BF16),
        V((8, 2, 256, 128), BF16),
        V((8, 256, 128), BF16),
        V((8, 256, 128), BF16),
        V((8, 8, 128), F32),
        V((8, 8, 128), F32),
        V((8, 256, 128), F32),
        V((2, 4, 2, 128, 128), BF16),
        V((2, 4, 2, 128, 128), BF16),
        V((4, 2, 128, 128), BF16),
        V((256, 128), F32),
        V((3, 128, 512), BF16),
        V((3, 128, 512), BF16),
        V((3, 128, 512), F32),
        V((3, 128, 512), BF16),
        V((3, 7, 16, 512), BF16),
        V((16, 512), BF16),
        V((3, 16, 512), BF16),
        V((256, 128), F32),
        V((16, 512), BF16),
        V((7, 16, 512), BF16),
        V((16, 512), BF16),
        V((15, 16, 512), BF16),
        V((16, 512), BF16),
        V((7, 16, 512), BF16),
        V((16, 128), F32),
        V((16, 128), F32),
        V((3, 16, 128), F32),
        V((3, 64, 128), F32),
        D((8, 4)),
        D((11,)),
        D((8,)),
        D((3,)),
        D((8, 2)),
        D((8, 2)),
        D((8, 2)),
        D((8, 2)),
        D((8,)),
        D((8,)),
        D((2,)),
        D((2, 4, 2)),
        D((2, 4, 2)),
        D((2, 3)),
        D((2, 3)),
        D((3,)),
        D((3,)),
        D((3,)),
        D((3,)),
        D((7,)),
        D((7,)),
    ]
    return pl.pallas_call(
        kernel,
        out_shape=(
            jax.ShapeDtypeStruct((8, 256, 128), F32),
            jax.ShapeDtypeStruct((1, 256, 128), F32),
            jax.ShapeDtypeStruct((1, 256, 128), F32),
            jax.ShapeDtypeStruct((3, 64, 128), F32),
        ),
        in_specs=[smem] * 3 + [anywhere] * 13,
        out_specs=(anywhere,) * 4,
        scratch_shapes=scratch,
        compiler_params=pltpu.CompilerParams(
            collective_id=0, has_side_effects=True, vmem_limit_bytes=48 * 1024 * 1024
        ),
        name="tree_solve",
    )(
        leaf_parent, leaf_pattern, mid_pattern, leaf_rhs, leaf_inv, leaf_lower_mid,
        leaf_lower_coupling, mid_rhs, parent_diagonal_inverse, mid_lower, top_rhs, top_inv,
        top_lower, apex_rhs, apex_inv, apex_lower,
    )


def solution(mesh):
    placed = (
        P(("gz", "col"), None, None),
        P(("gz", "col"), "row", None),
        P(("gz", "col"), None, "row"),
        P(("gz", "col"), None, None, "row"),
        P(("gz", "col")),
        P(("gz", "col"), None),
        P(("gz", "col"), None, None),
        P(("gz", "col"), "row", None),
        P(("gz", "col"), None, None, "row"),
        P(("gz", "col"), None),
        P("gz", None, None),
        P("gz", "row", None),
        P("gz", None, None, "row"),
        P(),
        P(None, "row", None),
        P(None, None, "row"),
    )
    return jax.shard_map(
        per_device,
        mesh=mesh,
        in_specs=placed,
        out_specs=(
            P(("gz", "col"), None, "row"),
            P(("gz", "col"), None, "row"),
            P("gz", None, "row"),
            P(None, "gz", "row"),
        ),
        check_vma=False,
    )
```

time: 480 us -> 99.3 us (0.21)
  waiting for transfers between devices: 388 us -> 0 us
  Pallas kernels: 0 us -> 82 us
  matrix products: 53.2 us -> 0 us
  between operations: 14 us -> 0.65 us
  starting transfers between devices: 7.14 us -> 0 us
  local copies, waits for them, and re-layouts: 9.66 us -> 15.2 us
    psum x4 -> x0, waiting for transfers between devices: 311 us -> none  [the longest x1 189 us: per_device(): layer_full = lax.psum(layer_part, ('row', 'col'))]
    pallas_call x0 -> x1, Pallas kernels: none -> 82 us  [per_device(): pl.pallas_call(kernel, out_shape=(jax.ShapeDtypeStruct((8, 256, 128), F32...]
    reduce_scatter x1 -> x0, waiting for transfers between devices: 63.3 us -> none  [per_device(): summed = lax.psum_scatter(mid_terms, 'col', scatter_dimension=0, tiled=True)]
    dot_general x12 -> x0, matrix products: 53.2 us -> none  [the longest x1 22.7 us: per_device(): jnp.einsum('lk,lkra->kra', up_weight, to_up, precision=lax.Precision.HIGH...]
    unnamed x20 -> x29, local copies, waits for them, and re-layouts: 1.59 us -> 15.2 us
    ppermute x3 -> x0, waiting for transfers between devices: 13.3 us -> none  [from_partner(): return lax.ppermute(block, axis, route)]
    dot_general x1 -> x0, local copies, waits for them, and re-layouts: 8.07 us -> none  [per_device(): jnp.einsum('lm,lra->mra', onehot, toward_parent, precision=lax.Precision....]
    ppermute x3 -> x0, starting transfers between devices: 6.76 us -> none  [from_partner(): return lax.ppermute(block, axis, route)]
  transfers between devices with their start and end apart: 8 -> 0, of which waited for: 7 -> 0; matrix products, arithmetic and copies ran while one was open for 7% -> 0% of each run, Pallas kernels for 0% -> 0%
where the time goes in v1:
time: 99.3 us; the launch traced here: 97.9 us
  Pallas kernels  82 us (83%)
  local copies, waits for them, and re-layouts  15.2 us (15%)
    pallas_call x1, Pallas kernels, per_device(): pl.pallas_call(kernel, out_shape=(jax.ShapeDtypeStruct((8, 256, 128), F32...  82 us
    unnamed x29, local copies, waits for them, and re-layouts  15.2 us

profile of v1, /device:TPU:1, one launch (start us, length us, event | category | flops | bytes accessed | tf_op | source)
XLA Modules:
  0.0 97.9 jit_solution(15204260697738540638)
XLA Ops:
  0.6 0.8 copy.20.pattern_s
  1.4 0.0 copy-start
  1.4 1.2 %copy-done = bf16[8,128,512]{2,1,0:T(8,128)(2,1)S(1)} copy-done((bf16[8,128,512]{2,1,0:T(8,128)(2,1)S(1)}, bf16[8,128,512]{2,1,0:T(8,128)(2,1)}, u32[]{:S(2)}) %copy-start) | copy-done | bytes 1048600
  2.6 0.0 copy-start.1
  2.6 1.2 %copy-done.1 = bf16[8,512,128]{2,1,0:T(8,128)(2,1)S(1)} copy-done((bf16[8,512,128]{2,1,0:T(8,128)(2,1)S(1)}, bf16[8,512,128]{2,1,0:T(8,128)(2,1)}, u32[]{:S(2)}) %copy-start.1) | copy-done | bytes 1048600
  3.8 0.0 copy-start.2
  3.8 1.0 %copy-done.2 = f32[1,256,512]{2,1,0:T(8,128)S(1)} copy-done((f32[1,256,512]{2,1,0:T(8,128)S(1)}, f32[1,256,512]{2,1,0:T(8,128)}, u32[]{:S(2)}) %copy-start.2) | copy-done | bytes 524312
  4.9 0.0 copy-start.3
  4.9 1.0 %copy-done.3 = f32[1,256,512]{2,1,0:T(8,128)S(1)} copy-done((f32[1,256,512]{2,1,0:T(8,128)S(1)}, f32[1,256,512]{2,1,0:T(8,128)}, u32[]{:S(2)}) %copy-start.3) | copy-done | bytes 524312
  5.9 0.0 copy-start.4
  5.9 1.0 %copy-done.4 = bf16[1,3,512,128]{3,2,1,0:T(8,128)(2,1)S(1)} copy-done((bf16[1,3,512,128]{3,2,1,0:T(8,128)(2,1)S(1)}, bf16[1,3,512,128]{3,2,1,0:T(8,128)(2,1)}, u32[]{:S(2)}) %copy-start.4) | copy-done | bytes 393240
  6.9 0.0 copy-start.5
  6.9 1.0 %copy-done.5 = bf16[3,128,512]{2,1,0:T(8,128)(2,1)S(1)} copy-done((bf16[3,128,512]{2,1,0:T(8,128)(2,1)S(1)}, bf16[3,128,512]{2,1,0:T(8,128)(2,1)}, u32[]{:S(2)}) %copy-start.5) | copy-done | bytes 393240
  7.9 0.0 copy-start.6
  7.9 0.9 copy-done.6
  8.9 0.0 copy-start.7
  8.9 0.9 copy-done.7
  9.8 0.0 copy-start.8
  9.8 0.9 copy-done.8
  10.7 0.0 copy-start.9
  10.7 0.9 copy-done.9
  11.6 0.0 copy-start.10
  11.6 0.7 copy-done.10
  12.3 0.0 copy-start.11
  12.3 0.7 copy-done.11
  12.9 82.0 %tree_solve.1 = (f32[8,256,128]{2,1,0:T(8,128)S(1)}, f32[1,256,128]{2,1,0:T(8,128)S(1)}, f32[1,256,128]{2,1,0:T(8,128)S(1)}, f32[3,64,128]{2,1,0:T(8,128)S(1)}) custom-call(s32[8]{0:T(128)S(1)} %copy-done.10, s32[8,3]{1,0:T(8,128)S(1)} %copy.20.pattern_s, s32[1,2]{1,0:T(1,128)S(1)} %copy-done.11, f32[8,256,512]{2,1,0:T(8,128)} %rhs_h.1, ...), custom_call_target="tpu_custom_call" | custom-call | tf_op jit(solution)/shard_map/tree_solve/pallas_call | solution.py:594
  94.9 1.0 copy.25
  95.9 0.7 copy.26
  96.6 0.7 copy.27
  97.2 0.6 copy.28
Async XLA Ops:
  1.4 1.2 %copy-start = (bf16[8,128,512]{2,1,0:T(8,128)(2,1)S(1)}, bf16[8,128,512]{2,1,0:T(8,128)(2,1)}, u32[]{:S(2)}) copy-start(bf16[8,128,512]{2,1,0:T(8,128)(2,1)} %inv_h.1) | copy-start | bytes 3145732
  2.6 1.2 %copy-start.1 = (bf16[8,512,128]{2,1,0:T(8,128)(2,1)S(1)}, bf16[8,512,128]{2,1,0:T(8,128)(2,1)}, u32[]{:S(2)}) copy-start(bf16[8,512,128]{2,1,0:T(8,128)(2,1)} %lm_h.1) | copy-start | bytes 3145732
  3.8 1.0 %copy-start.2 = (f32[1,256,512]{2,1,0:T(8,128)S(1)}, f32[1,256,512]{2,1,0:T(8,128)}, u32[]{:S(2)}) copy-start(f32[1,256,512]{2,1,0:T(8,128)} %midrhs_h.1) | copy-start | bytes 1572868
  4.9 1.0 %copy-start.3 = (f32[1,256,512]{2,1,0:T(8,128)S(1)}, f32[1,256,512]{2,1,0:T(8,128)}, u32[]{:S(2)}) copy-start(f32[1,256,512]{2,1,0:T(8,128)} %toprhs_h.1) | copy-start | bytes 1572868
  5.9 1.0 %copy-start.4 = (bf16[1,3,512,128]{3,2,1,0:T(8,128)(2,1)S(1)}, bf16[1,3,512,128]{3,2,1,0:T(8,128)(2,1)}, u32[]{:S(2)}) copy-start(bf16[1,3,512,128]{3,2,1,0:T(8,128)(2,1)} %midl_h.1) | copy-start | bytes 1179652
  6.9 1.0 %copy-start.5 = (bf16[3,128,512]{2,1,0:T(8,128)(2,1)S(1)}, bf16[3,128,512]{2,1,0:T(8,128)(2,1)}, u32[]{:S(2)}) copy-start(bf16[3,128,512]{2,1,0:T(8,128)(2,1)} %apexinv_h.1) | copy-start | bytes 1179652
  7.9 0.9 copy-start.6
  8.9 0.9 copy-start.7
  9.8 0.9 copy-start.8
  10.7 0.9 copy-start.9
  11.6 0.7 copy-start.10
  12.3 0.7 copy-start.11

commit v2 on v1

v2 whole, which is shorter than its diff:
```python
import jax
import jax.numpy as jnp
from jax import lax
from jax.experimental import pallas as pl
from jax.experimental.pallas import tpu as pltpu
from jax.sharding import PartitionSpec as P

MESH = pl.DeviceIdType.MESH
F32 = jnp.float32
BF16 = jnp.bfloat16
N_LEAF = 8
SLICE = 128
HALF = 128
ROWS_Y = 128
ROWS_Z = 256 - ROWS_Y
SHARE = 16


def dot_nt(a, b):
    return lax.dot_general(a, b, (((1,), (1,)), ((), ())), preferred_element_type=F32)


def send(src, dst, send_sem, recv_sem, where):
    return pltpu.make_async_remote_copy(
        src_ref=src,
        dst_ref=dst,
        send_sem=send_sem,
        recv_sem=recv_sem,
        device_id=where,
        device_id_type=MESH,
    )


def kernel(
    parent_s,
    pattern_s,
    midpat_s,
    rhs_h,
    inv_h,
    lm_h,
    lc_h,
    midrhs_h,
    pinv_h,
    midl_h,
    toprhs_h,
    topinv_h,
    topl_h,
    apexrhs_h,
    apexinv_h,
    apexl_h,
    leaf_o,
    mid_o,
    top_o,
    apex_o,
    rhs_v,
    inv_v,
    lm_v,
    lc_v,
    midrhs_v,
    pinv_v,
    midl_v,
    toprhs_v,
    topinv_v,
    topl_v,
    apexrhs_v,
    apexinv_v,
    apexl_v,
    sol_v,
    rnd_v,
    weight_v,
    pidrow_v,
    up_v,
    yopp_v,
    y1_v,
    ysend_v,
    y2_v,
    part_v,
    sib_v,
    pid_v,
    pidsib_v,
    acc_v,
    yz_s,
    yz_r,
    pairs_s,
    pairs_r,
    wide_v,
    zsum_s,
    zsum_r,
    rs_s,
    rs_r,
    mt_v,
    msol_v,
    csend_v,
    crecv_v,
    ownp_v,
    zsc_v,
    zin_v,
    rsend_v,
    rrecv_v,
    tops_v,
    q1_v,
    q1r_v,
    e_v,
    er_v,
    u_v,
    ur_v,
    fsend_v,
    fother_v,
    fins_v,
    fin_v,
    ld_leaf,
    ld_misc,
    out_leaf,
    out_misc,
    y1_ss,
    y1_rs,
    y2_ss,
    y2_rs,
    sib_ss,
    sib_rs,
    pid_sem,
    pairs_ss,
    pairs_rs,
    yz_sem,
    zsum_ss,
    zsum_rs,
    rs_ss,
    rs_rs,
    mt_ss,
    mt_rs,
    c_ss,
    c_rs,
    zin_ss,
    zin_rs,
    x_ss,
    x_rs,
):
    g = lax.axis_index("gz")
    r = lax.axis_index("row")
    c = lax.axis_index("col")
    z, core = c // 2, c % 2
    pair = g // 2
    mate = g + 1 - 2 * (g % 2)
    facing = 3 - g
    block = core * 128 + z * SHARE
    sibling = {"col": 2 * z + (1 - core)}
    ahead, behind, across = (r + 1) % 4, (r + 3) % 4, (r + 2) % 4
    y_half, z_half = ROWS_Y // 2, ROWS_Z // 2

    def rows(start, count, unit):
        return pl.ds(pl.multiple_of(start, unit), count)

    def slab(index):
        return rows(index * SLICE, SLICE, SLICE)

    barrier = pltpu.get_barrier_semaphore()

    def greet(where):
        pl.semaphore_signal(barrier, inc=1, device_id=where, device_id_type=MESH)

    greet(sibling)
    for apart in range(1, 8):
        greet({"col": 2 * ((z + apart) % 8) + core})
    for apart in range(1, 4):
        greet({"row": (r + apart) % 4})
    for apart in range(4):
        greet({"gz": mate, "row": (r + apart) % 4})
        greet({"gz": facing, "row": (r + apart) % 4})
    greet({"gz": (g + 2) % 4})
    for i in range(4):
        giver = 2 * ((g % 2) * 4 + i) + g // 2
        greet({"gz": (g + 1 + ((c - giver + 16) % 16) // 4) % 4, "col": giver})

    def leaf_loads(l):
        return (
            pltpu.make_async_copy(rhs_h.at[l], rhs_v.at[l], ld_leaf.at[l, 0]),
            pltpu.make_async_copy(inv_h.at[l], inv_v.at[l], ld_leaf.at[l, 1]),
        )

    def lower_load(l):
        return pltpu.make_async_copy(lm_h.at[l], lm_v.at[:, slab(l)], ld_leaf.at[l, 2])

    def coupling_load(l):
        return pltpu.make_async_copy(lc_h.at[l], lc_v.at[:, :, slab(l)], ld_leaf.at[l, 3])

    misc = (
        (midrhs_h.at[0, :, slab(r)], midrhs_v),
        (pinv_h.at[0], pinv_v),
        (midl_h.at[0], midl_v),
        (toprhs_h.at[0, rows(block, SHARE, SHARE), :], toprhs_v),
        (topinv_h.at[0], topinv_v),
        (topl_h.at[0], topl_v),
        (apexrhs_h.at[pair, rows(block, SHARE, SHARE), :], apexrhs_v.at[0]),
        (apexrhs_h.at[2, rows(block, SHARE, SHARE), :], apexrhs_v.at[1]),
        (apexinv_h.at[pair], apexinv_v.at[0]),
        (apexinv_h.at[2], apexinv_v.at[1]),
        (apexl_h.at[pair], apexl_v),
    )
    misc = [pltpu.make_async_copy(s, d, ld_misc.at[i]) for i, (s, d) in enumerate(misc)]

    @pl.loop(0, N_LEAF)
    def _(l):
        for copy in leaf_loads(l):
            copy.start()

    @pl.loop(0, N_LEAF)
    def _(l):
        lower_load(l).start()

    @pl.loop(0, N_LEAF)
    def _(l):
        coupling_load(l).start()

    for copy in misc:
        copy.start()

    @pl.loop(0, N_LEAF)
    def _(l):
        parent = parent_s[l].astype(F32)
        pid_v[l] = jnp.full((8, 128), parent, F32)
        pidrow_v[:, slab(l)] = jnp.full((16, 128), parent, F32)
        for k in range(3):
            weight_v[k, :, slab(l)] = jnp.full((16, 128), pattern_s[k, l].astype(F32), F32).astype(
                BF16
            )

    def leaf_out(l):
        return pltpu.make_async_copy(sol_v.at[l], leaf_o.at[l], out_leaf.at[l])

    @pl.loop(0, N_LEAF)
    def _(l):
        for copy in leaf_loads(l):
            copy.wait()
        solved = dot_nt(rhs_v[l].astype(BF16), inv_v[l])
        sol_v[l] = solved
        rnd_v[:, slab(l)] = solved.astype(BF16)
        leaf_out(l).start()

    pl.semaphore_wait(barrier, 24)

    pid_copy = send(pid_v, pidsib_v, pid_sem.at[0], pid_sem.at[1], sibling)
    pid_copy.start()

    def y1_copies(l):
        return (
            send(
                yopp_v.at[l, pl.ds(0, y_half)], y1_v.at[l, 0], y1_ss.at[l, 0], y1_rs.at[l, 0],
                {"row": ahead},
            ),
            send(
                yopp_v.at[l, pl.ds(y_half, y_half)], y1_v.at[l, 1], y1_ss.at[l, 1],
                y1_rs.at[l, 1], {"row": behind},
            ),
        )

    def y2_copies(l):
        return (
            send(ysend_v.at[l, 0], y2_v.at[l, 0], y2_ss.at[l, 0], y2_rs.at[l, 0], {"row": ahead}),
            send(ysend_v.at[l, 1], y2_v.at[l, 1], y2_ss.at[l, 1], y2_rs.at[l, 1], {"row": behind}),
        )

    def sib_copy(l):
        return send(part_v.at[l], sib_v.at[l], sib_ss.at[l], sib_rs.at[l], sibling)

    def to_mid(l, target):
        return dot_nt(rnd_v[:ROWS_Y, slab(l)], lm_v[slab(target), slab(l)])

    @pl.loop(0, N_LEAF)
    def _(l):
        lower_load(l).wait()
        yopp_v[l] = to_mid(l, across).astype(BF16)
        for copy in y1_copies(l):
            copy.start()

    def pairs_copy(t):
        return send(pairs_s.at[t], pairs_r.at[t], pairs_ss.at[t], pairs_rs.at[t], sibling)

    def masked(parent):
        hit = jnp.maximum(1.0 - jnp.abs(pidrow_v[...] - parent.astype(F32)), 0.0).astype(BF16)
        terms = rnd_v[ROWS_Y:].reshape(ROWS_Z // 16, 16, 1024) * hit[None]
        return terms.reshape(ROWS_Z, 1024)

    def in_turn(i):
        return (z + 4 + ((i + 1) // 2) * (1 - 2 * (i % 2))) % 8

    def pairs(first, last):
        @pl.loop(first, last)
        def _(i):
            t = in_turn(i)
            terms = jnp.concatenate([masked(2 * t + 1 - core), masked(2 * t + core)], axis=0)
            sums = dot_nt(terms, lm_v[...])
            pairs_s[t] = sums[:ROWS_Z].astype(BF16)
            pairs_copy(t).start()
            wide_v[t] = sums[ROWS_Z:]

    pairs(0, 3)

    def z_copy(buffers, way, dist, h):
        out, into, send_sem, recv_sem = buffers
        at = (way, dist - 1, h)
        step = 1 if way == 0 else 7
        return send(
            out.at[at], into.at[at], send_sem.at[at], recv_sem.at[at],
            {"col": 2 * ((z + step) % 8) + core},
        )

    zsum = (zsum_s, zsum_r, zsum_ss, zsum_rs)
    flows = [
        (way, dist, way if late else 1 - way)
        for dist in (4, 3, 2, 1)
        for late in (0, 1)
        for way in (0, 1)
        if late or dist < 4
    ]

    def z_step(buffers, term_of, group):
        for way, dist, h in group:
            target = (z + dist) % 8 if way == 0 else (z + 8 - dist) % 8
            term = term_of(target, h)
            if (way, dist + 1, h) in flows:
                z_copy(buffers, way, dist + 1, h).wait_recv()
                term = term + buffers[1][way, dist, h].astype(F32)
            buffers[0][way, dist - 1, h] = term.astype(BF16)
            z_copy(buffers, way, dist, h).start()

    def z_term(target, h):
        part = pl.ds(h * z_half, z_half)
        return wide_v[target, part] + pairs_r[target, part].astype(F32)

    def ready(t):
        pairs_copy(t % 8).wait_recv()

    ready(z + 4)
    z_step(zsum, z_term, flows[0:2])
    ready(z + 3)
    ready(z + 5)
    z_step(zsum, z_term, flows[2:4])

    @pl.loop(0, N_LEAF)
    def _(l):
        forward, backward = y1_copies(l)
        to_ahead, to_behind = y2_copies(l)
        term = to_mid(l, ahead)
        forward.wait_recv()
        ysend_v[l, 0, :y_half] = (term[:y_half] + y1_v[l, 0].astype(F32)).astype(BF16)
        ysend_v[l, 0, y_half:] = term[y_half:].astype(BF16)
        to_ahead.start()
        term = to_mid(l, behind)
        backward.wait_recv()
        ysend_v[l, 1, :y_half] = term[:y_half].astype(BF16)
        ysend_v[l, 1, y_half:] = (term[y_half:] + y1_v[l, 1].astype(F32)).astype(BF16)
        to_behind.start()

    pairs(3, 8)
    z_step(zsum, z_term, flows[4:6])

    @pl.loop(0, N_LEAF)
    def _(l):
        coupling_load(l).wait()

    for k in range(3):
        terms = rnd_v[...].reshape(16, 16, 1024) * weight_v[k][None]
        up_v[k] = dot_nt(terms.reshape(256, 1024), lc_v[k])

    ready(z + 2)
    ready(z + 6)
    z_step(zsum, z_term, flows[6:8])

    acc_v[...] = jnp.zeros_like(acc_v)

    def gather_parents(pids, terms):
        for t in range(8):
            wanted = (2 * t + core).astype(F32)
            hit = jnp.maximum(1.0 - jnp.abs(pids - wanted), 0.0)
            acc_v[t] += (terms.reshape(ROWS_Y // 8, 8, 128) * hit[None]).reshape(ROWS_Y, 128)

    def collect(first, last):
        @pl.loop(first, last)
        def _(l):
            term = to_mid(l, r)
            for copy in y2_copies(l):
                copy.wait_recv()
            total = term + y2_v[l, 0].astype(F32) + y2_v[l, 1].astype(F32)
            part_v[l] = total.astype(BF16)
            sib_copy(l).start()
            gather_parents(pid_v[l], total)

            @pl.when(l > 0)
            def _():
                sib_copy(l - 1).wait_recv()
                gather_parents(pidsib_v[l - 1], sib_v[l - 1].astype(F32))

    pid_copy.wait_recv()
    collect(0, 3)
    z_step(zsum, z_term, flows[8:10])
    collect(3, 6)
    ready(z + 1)
    ready(z + 7)
    z_step(zsum, z_term, flows[10:12])
    collect(6, N_LEAF)
    sib_copy(N_LEAF - 1).wait_recv()
    gather_parents(pidsib_v[N_LEAF - 1], sib_v[N_LEAF - 1].astype(F32))

    def yz_copy(apart):
        target = (z + apart) % 8
        return send(
            yz_s.at[target], yz_r.at[apart - 1], yz_sem.at[0], yz_sem.at[1],
            {"col": 2 * target + core},
        )

    yz_all = send(yz_r, yz_r, yz_sem.at[0], yz_sem.at[1], sibling)
    for apart in (4, 3, 5, 2, 6, 1, 7):
        target = (z + apart) % 8
        yz_s[target] = acc_v[target].astype(BF16)
        yz_copy(apart).start()
    z_step(zsum, z_term, flows[12:14])

    def rs_copy(apart):
        return send(
            rs_s.at[(r + apart) % 4], rs_r.at[apart - 1], rs_ss.at[apart - 1],
            rs_rs.at[apart - 1], {"row": (r + apart) % 4},
        )

    ready(z)
    for h in (0, 1):
        for way in (0, 1):
            z_copy(zsum, way, 1, h).wait_recv()
        total = z_term(z, h) + zsum_r[0, 0, h].astype(F32) + zsum_r[1, 0, h].astype(F32)
        wide_v[z, h * z_half : (h + 1) * z_half] = total
        for i in range(4):
            rs_s[i, h * z_half : (h + 1) * z_half] = total[:, i * SLICE : (i + 1) * SLICE].astype(
                BF16
            )
    for apart in (2, 1, 3):
        rs_copy(apart).start()

    parts = ((0, ROWS_Y), (ROWS_Y, ROWS_Z))

    def mt_copy(p, apart):
        mine = mt_v.at[r, pl.ds(*parts[p])]
        return send(
            mine, mine, mt_ss.at[p, apart - 1], mt_rs.at[p, apart - 1], {"row": (r + apart) % 4}
        )

    def mt_arrival(p, apart):
        source = (r + 4 - apart) % 4
        theirs = mt_v.at[source, pl.ds(*parts[p])]
        return send(
            theirs, theirs, mt_ss.at[p, apart - 1], mt_rs.at[p, apart - 1], {"row": source}
        )

    misc[0].wait()
    yz_all.wait_recv()
    total = midrhs_v[:ROWS_Y] - acc_v[z]
    for i in range(7):
        total = total - yz_r[i].astype(F32)
    mt_v[r, :ROWS_Y] = total.astype(BF16)
    for apart in (2, 1, 3):
        mt_copy(0, apart).start()
    for apart in (1, 2, 3):
        rs_copy(apart).wait_recv()
    total = midrhs_v[ROWS_Y:] - wide_v[z, :, slab(r)]
    for i in range(3):
        total = total - rs_r[i].astype(F32)
    mt_v[r, ROWS_Y:] = total.astype(BF16)
    for apart in (2, 1, 3):
        mt_copy(1, apart).start()

    mid_weight = (None, midpat_s[0, 0].astype(F32), midpat_s[0, 1].astype(F32))

    def c_copy(k):
        return send(csend_v.at[k], crecv_v.at[k], c_ss.at[k], c_rs.at[k], sibling)

    misc[1].wait()
    misc[2].wait()
    for h in (0, 1):
        for apart in (1, 2, 3):
            mt_arrival(h, apart).wait_recv()
        here = slice(h * HALF, (h + 1) * HALF)
        right = jnp.concatenate([mt_v[i, here] for i in range(4)], axis=1)
        solved = dot_nt(right, pinv_v[...])
        msol_v[here] = solved
        rounded = solved.astype(BF16)
        for k in range(3):
            term = dot_nt(rounded, midl_v[k])
            if k:
                term = term * mid_weight[k]
            up_v[k, here] = up_v[k, here] + term
            if h:
                csend_v[k] = up_v[k, rows((1 - core) * HALF, HALF, HALF)].astype(BF16)
                c_copy(k).start()
    mid_out = pltpu.make_async_copy(msol_v, mid_o.at[0], out_misc.at[0])
    mid_out.start()

    def zin_copy(k, apart):
        target = (z + apart) % 8
        return send(
            zsc_v.at[k, rows(target * SHARE, SHARE, SHARE)], zin_v.at[k, apart - 1],
            zin_ss.at[k], zin_rs.at[k], {"col": 2 * target + core},
        )

    def all_of(buffer, sem):
        return send(buffer, buffer, x_ss.at[sem], x_rs.at[sem], {"row": ahead})

    def zin_all(k):
        return send(zin_v.at[k], zin_v.at[k], zin_ss.at[k], zin_rs.at[k], {"row": ahead})

    for k in range(3):
        c_copy(k).wait_recv()
        total = up_v[k, rows(core * HALF, HALF, HALF)] + crecv_v[k].astype(F32)
        ownp_v[k] = total
        zsc_v[k] = total.astype(BF16)
        for apart in (4, 3, 5, 2, 6, 1, 7):
            zin_copy(k, apart).start()

    def share_sum(k):
        zin_all(k).wait_recv()
        total = ownp_v[k, rows(z * SHARE, SHARE, SHARE)]
        for i in range(7):
            total = total + zin_v[k, i].astype(F32)
        return total

    def to_rows(src, dst, sem):
        for apart in (2, 1, 3):
            send(
                src, dst.at[apart - 1], x_ss.at[sem], x_rs.at[sem], {"row": (r + apart) % 4}
            ).start()

    pid_copy.wait_send()

    @pl.loop(0, N_LEAF)
    def _(l):
        for copy in y1_copies(l) + y2_copies(l) + (sib_copy(l), pairs_copy(l)):
            copy.wait_send()
        leaf_out(l).wait()

    own = share_sum(0)
    rsend_v[...] = own.astype(BF16)
    to_rows(rsend_v, rrecv_v, 0)
    for i in range(3, 11):
        misc[i].wait()
    for way, dist, h in flows:
        z_copy(zsum, way, dist, h).wait_send()
    yz_all.wait_send()
    all_of(rrecv_v, 0).wait_recv()
    for i in range(3):
        own = own + rrecv_v[i].astype(F32)
    solved = dot_nt((toprhs_v[...] - own).astype(BF16), topinv_v[...])
    rounded = solved.astype(BF16)
    q1 = share_sum(1) + dot_nt(rounded, topl_v[0])
    q1_v[...] = q1.astype(BF16)

    def to_group(src, dst, sem, other):
        for layer in (1, 0):
            for apart in (2, 1, 3, 0):
                if layer or apart:
                    send(
                        src, dst.at[4 * layer + apart - 1], x_ss.at[sem], x_rs.at[sem],
                        {"gz": other if layer else g, "row": (r + apart) % 4},
                    ).start()

    to_group(q1_v, q1r_v, 1, mate)
    tops_v[rows(block, SHARE, SHARE)] = solved
    e = share_sum(2) + dot_nt(rounded, topl_v[1])
    e_v[0] = e.astype(BF16)
    to_rows(e_v.at[0], er_v.at[0], 2)
    for apart in range(1, 8):
        mine = tops_v.at[rows(block, SHARE, SHARE)]
        send(
            mine, mine, x_ss.at[3], x_rs.at[3], {"col": 2 * ((z + apart) % 8) + core}
        ).start()

    all_of(q1r_v, 1).wait_recv()
    for i in range(7):
        q1 = q1 + q1r_v[i].astype(F32)
    front = dot_nt((apexrhs_v[0] - q1).astype(BF16), apexinv_v[0])
    u = dot_nt(front.astype(BF16), apexl_v[...])
    u_v[...] = u.astype(BF16)
    to_group(u_v, ur_v, 4, facing)
    fsend_v[...] = front
    fins_v[pair] = front
    send(fsend_v, fother_v, x_ss.at[5], x_rs.at[5], {"gz": facing}).start()

    all_of(er_v.at[0], 2).wait_recv()
    for i in range(3):
        e = e + er_v[0, i].astype(F32)
    e_v[1] = e.astype(BF16)
    for apart in (1, 2, 3):
        send(
            e_v.at[1], er_v.at[1, apart - 1], x_ss.at[7], x_rs.at[7], {"gz": (g + apart) % 4}
        ).start()
    tops_seven = tops_v.at[rows(core * HALF, 112, HALF)]
    tops_eight = tops_v.at[rows(core * HALF, HALF, HALF)]
    tops_other = tops_v.at[rows((1 - core) * HALF, HALF, HALF)]
    all_of(tops_seven, 3).wait()
    tops_copy = send(tops_eight, tops_eight, x_ss.at[8], x_rs.at[8], sibling)
    tops_copy.start()
    for k in range(3):
        c_copy(k).wait_send()
        zin_all(k).wait_send()
    for p in (0, 1):
        for apart in (1, 2, 3):
            mt_copy(p, apart).wait_send()
    for apart in (1, 2, 3):
        rs_copy(apart).wait_send()
    all_of(rrecv_v, 0).wait_send()
    all_of(q1r_v, 1).wait_send()
    all_of(er_v.at[0], 2).wait_send()

    all_of(er_v.at[1], 7).wait_recv()
    for i in range(3):
        e = e + er_v[1, i].astype(F32)
    last = apexrhs_v[1] - e - u
    all_of(fother_v, 5).wait_recv()
    fins_v[1 - pair] = fother_v[...]
    all_of(ur_v, 4).wait_recv()
    for i in range(7):
        last = last - ur_v[i].astype(F32)
    fins_v[2] = dot_nt(last.astype(BF16), apexinv_v[1])

    holder = core * 2 + z // 4
    turn = (g - holder + 7) % 4
    for i in range(4):
        send(
            fins_v, fin_v.at[:, rows((z % 4) * SHARE, SHARE, SHARE)], x_ss.at[6], x_rs.at[6],
            {"gz": holder, "col": (c + 4 * turn + i) % 16},
        ).start()

    send(tops_eight, tops_other, x_ss.at[8], x_rs.at[8], sibling).wait_recv()
    top_out = pltpu.make_async_copy(tops_v, top_o.at[0], out_misc.at[1])
    top_out.start()
    tops_copy.wait_send()
    all_of(ur_v, 4).wait_send()
    all_of(fother_v, 5).wait_send()
    all_of(er_v.at[1], 7).wait_send()
    mid_out.wait()
    top_out.wait()
    all_of(fin_v, 6).wait()
    apex_out = pltpu.make_async_copy(fin_v, apex_o, out_misc.at[2])
    apex_out.start()
    apex_out.wait()


def place(leaf_i, mid_i, top_i, apex_i, leaf_o, mid_o, top_o, apex_o, sems):
    pairs = [(leaf_i.at[l], leaf_o.at[l]) for l in range(N_LEAF)]
    pairs += [(mid_i, mid_o), (top_i, top_o), (apex_i, apex_o)]
    copies = [pltpu.make_async_copy(s, d, sems.at[i]) for i, (s, d) in enumerate(pairs)]
    for copy in copies:
        copy.start()
    for copy in copies:
        copy.wait()


def per_device(*args):
    (
        leaf_rhs, leaf_inv, leaf_lower_mid, leaf_lower_coupling, leaf_parent, leaf_pattern,
        mid_rhs, parent_diagonal_inverse, mid_lower, mid_pattern, top_rhs, top_inv, top_lower,
        apex_rhs, apex_inv, apex_lower,
    ) = args
    smem = pl.BlockSpec(memory_space=pltpu.SMEM)
    anywhere = pl.BlockSpec(memory_space=pl.ANY)
    hbm = pl.BlockSpec(memory_space=pltpu.HBM)
    V = pltpu.VMEM
    D = pltpu.SemaphoreType.DMA
    scratch = [
        V((8, 256, 512), F32),
        V((8, 128, 512), BF16),
        V((512, 1024), BF16),
        V((3, 512, 1024), BF16),
        V((256, 128), F32),
        V((128, 512), BF16),
        V((3, 512, 128), BF16),
        V((16, 512), F32),
        V((128, 512), BF16),
        V((2, 512, 128), BF16),
        V((2, 16, 512), F32),
        V((2, 128, 512), BF16),
        V((512, 128), BF16),
        V((8, 256, 128), F32),
        V((256, 1024), BF16),
        V((3, 16, 1024), BF16),
        V((16, 1024), F32),
        V((3, 256, 512), F32),
        V((8, ROWS_Y, 128), BF16),
        V((8, 2, ROWS_Y // 2, 128), BF16),
        V((8, 2, ROWS_Y, 128), BF16),
        V((8, 2, ROWS_Y, 128), BF16),
        V((8, ROWS_Y, 128), BF16),
        V((8, ROWS_Y, 128), BF16),
        V((8, 8, 128), F32),
        V((8, 8, 128), F32),
        V((8, ROWS_Y, 128), F32),
        V((8, ROWS_Y, 128), BF16),
        V((7, ROWS_Y, 128), BF16),
        V((8, ROWS_Z, 512), BF16),
        V((8, ROWS_Z, 512), BF16),
        V((8, ROWS_Z, 512), F32),
        V((2, 4, 2, ROWS_Z // 2, 512), BF16),
        V((2, 4, 2, ROWS_Z // 2, 512), BF16),
        V((4, ROWS_Z, 128), BF16),
        V((3, ROWS_Z, 128), BF16),
        V((4, 256, 128), BF16),
        V((256, 128), F32),
        V((3, 128, 512), BF16),
        V((3, 128, 512), BF16),
        V((3, 128, 512), F32),
        V((3, 128, 512), BF16),
        V((3, 7, 16, 512), BF16),
        V((16, 512), BF16),
        V((3, 16, 512), BF16),
        V((256, 128), F32),
        V((16, 512), BF16),
        V((7, 16, 512), BF16),
        V((2, 16, 512), BF16),
        V((2, 3, 16, 512), BF16),
        V((16, 512), BF16),
        V((7, 16, 512), BF16),
        V((16, 128), F32),
        V((16, 128), F32),
        V((3, 16, 128), F32),
        V((3, 64, 128), F32),
        D((8, 4)),
        D((11,)),
        D((8,)),
        D((3,)),
        D((8, 2)),
        D((8, 2)),
        D((8, 2)),
        D((8, 2)),
        D((8,)),
        D((8,)),
        D((2,)),
        D((8,)),
        D((8,)),
        D((2,)),
        D((2, 4, 2)),
        D((2, 4, 2)),
        D((3,)),
        D((3,)),
        D((2, 3)),
        D((2, 3)),
        D((3,)),
        D((3,)),
        D((3,)),
        D((3,)),
        D((9,)),
        D((9,)),
    ]
    solved = pl.pallas_call(
        kernel,
        out_shape=(
            jax.ShapeDtypeStruct((8, 256, 128), F32),
            jax.ShapeDtypeStruct((1, 256, 128), F32),
            jax.ShapeDtypeStruct((1, 256, 128), F32),
            jax.ShapeDtypeStruct((3, 64, 128), F32),
        ),
        in_specs=[smem] * 3 + [hbm] * 13,
        out_specs=(anywhere,) * 4,
        scratch_shapes=scratch,
        compiler_params=pltpu.CompilerParams(
            collective_id=0, has_side_effects=True, vmem_limit_bytes=56 * 1024 * 1024
        ),
        name="tree_solve",
    )(
        leaf_parent, leaf_pattern.T, mid_pattern, leaf_rhs, leaf_inv, leaf_lower_mid,
        leaf_lower_coupling, mid_rhs, parent_diagonal_inverse, mid_lower, top_rhs, top_inv,
        top_lower, apex_rhs, apex_inv, apex_lower,
    )
    return pl.pallas_call(
        place,
        out_shape=[jax.ShapeDtypeStruct(x.shape, x.dtype) for x in solved],
        in_specs=[pl.BlockSpec(memory_space=V)] * 4,
        out_specs=[anywhere] * 4,
        scratch_shapes=[D((11,))],
        compiler_params=pltpu.CompilerParams(vmem_limit_bytes=56 * 1024 * 1024),
        name="place",
    )(*solved)


def solution(mesh):
    placed = (
        P(("gz", "col"), None, None),
        P(("gz", "col"), "row", None),
        P(("gz", "col"), None, "row"),
        P(("gz", "col"), None, None, "row"),
        P(("gz", "col")),
        P(("gz", "col"), None),
        P(("gz", "col"), None, None),
        P(("gz", "col"), "row", None),
        P(("gz", "col"), None, None, "row"),
        P(("gz", "col"), None),
        P("gz", None, None),
        P("gz", "row", None),
        P("gz", None, None, "row"),
        P(),
        P(None, "row", None),
        P(None, None, "row"),
    )
    return jax.shard_map(
        per_device,
        mesh=mesh,
        in_specs=placed,
        out_specs=(
            P(("gz", "col"), None, "row"),
            P(("gz", "col"), None, "row"),
            P("gz", None, "row"),
            P(None, "gz", "row"),
        ),
        check_vma=False,
    )
```

time: 99.3 us -> 78.7 us (0.79); the launches traced: 97.9 us -> 78.2 us
  local copies, waits for them, and re-layouts: 15.2 us -> 0 us
  Pallas kernels: 82 us -> 77.6 us
    unnamed x29 -> x0, local copies, waits for them, and re-layouts: 15.2 us -> none
    pallas_call x1, Pallas kernels: 82 us -> 75.1 us  [per_device(): pl.pallas_call(kernel, out_shape=(jax.ShapeDtypeStruct((8, 256, 128), F32...]
    pallas_call x0 -> x1, Pallas kernels: none -> 2.48 us  [per_device(): pl.pallas_call(place, out_shape=[jax.ShapeDtypeStruct(x.shape, x.dtype) f...]
where the time goes in v2:
time: 78.7 us; the launch traced here: 78.2 us
  Pallas kernels  77.6 us (99%)
    pallas_call x1, Pallas kernels, per_device(): pl.pallas_call(kernel, out_shape=(jax.ShapeDtypeStruct((8, 256, 128), F32...  75.1 us
    pallas_call x1, Pallas kernels, per_device(): pl.pallas_call(place, out_shape=[jax.ShapeDtypeStruct(x.shape, x.dtype) f...  2.48 us

profile of v2, /device:TPU:1, one launch (start us, length us, event | category | flops | bytes accessed | tf_op | source)
XLA Modules:
  0.0 78.2 jit_solution(10832061780115120383)
XLA Ops:
  0.6 75.1 %tree_solve.1 = (f32[8,256,128]{2,1,0:T(8,128)}, f32[1,256,128]{2,1,0:T(8,128)}, f32[1,256,128]{2,1,0:T(8,128)}, f32[3,64,128]{2,1,0:T(8,128)}) custom-call(s32[8]{0:T(128)} %parent_s.1, s32[3,8]{1,0:T(4,128)} %bitcast.1, s32[1,2]{1,0:T(1,128)} %midpat_s.1, f32[8,256,512]{2,1,0:T(8,128)} %rhs_h.1, bf16[8,128,512]{2,1,0:T(8,128)(2,1)} %inv_h.1, ...), custom_call_target="tpu_custom_call" | custom-call | tf_op jit(solution)/shard_map/tree_solve/pallas_call | solution.py:749
  75.8 2.5 %place.1 = (f32[8,256,128]{2,1,0:T(8,128)}, f32[1,256,128]{2,1,0:T(8,128)}, f32[1,256,128]{2,1,0:T(8,128)}, f32[3,64,128]{2,1,0:T(8,128)}) custom-call(f32[8,256,128]{2,1,0:T(8,128)} %get-tuple-element.8.leaf_i, f32[1,256,128]{2,1,0:T(8,128)} %get-tuple-element.9.mid_i, f32[1,256,128]{2,1,0:T(8,128)} %get-tuple-element.10.top_i, ...), custom_call_target="tpu_custom_call" | custom-call | tf_op jit(solution)/shard_map/place/pallas_call | solution.py:769

commit v3 on v2

--- a/solution.py
+++ b/solution.py
@@ -11,8 +11,9 @@
 N_LEAF = 8
 SLICE = 128
 HALF = 128
-ROWS_Y = 128
+ROWS_Y = 64
 ROWS_Z = 256 - ROWS_Y
+PIECES = (48, 48, 48, 48)
 SHARE = 16
 
 
@@ -70,10 +71,9 @@
     weight_v,
     pidrow_v,
     up_v,
-    yopp_v,
-    y1_v,
-    ysend_v,
-    y2_v,
+    y_s,
+    y_own,
+    y_r,
     part_v,
     sib_v,
     pid_v,
@@ -88,6 +88,8 @@
     zsum_r,
     rs_s,
     rs_r,
+    last_s,
+    last_r,
     mt_v,
     msol_v,
     csend_v,
@@ -112,10 +114,8 @@
     ld_misc,
     out_leaf,
     out_misc,
-    y1_ss,
-    y1_rs,
-    y2_ss,
-    y2_rs,
+    y_ss,
+    y_rs,
     sib_ss,
     sib_rs,
     pid_sem,
@@ -124,8 +124,9 @@
     yz_sem,
     zsum_ss,
     zsum_rs,
-    rs_ss,
-    rs_rs,
+    rs_sem,
+    last_ss,
+    last_rs,
     mt_ss,
     mt_rs,
     c_ss,
@@ -144,32 +145,13 @@
     facing = 3 - g
     block = core * 128 + z * SHARE
     sibling = {"col": 2 * z + (1 - core)}
-    ahead, behind, across = (r + 1) % 4, (r + 3) % 4, (r + 2) % 4
-    y_half, z_half = ROWS_Y // 2, ROWS_Z // 2
+    ahead = (r + 1) % 4
 
     def rows(start, count, unit):
         return pl.ds(pl.multiple_of(start, unit), count)
 
     def slab(index):
         return rows(index * SLICE, SLICE, SLICE)
-
-    barrier = pltpu.get_barrier_semaphore()
-
-    def greet(where):
-        pl.semaphore_signal(barrier, inc=1, device_id=where, device_id_type=MESH)
-
-    greet(sibling)
-    for apart in range(1, 8):
-        greet({"col": 2 * ((z + apart) % 8) + core})
-    for apart in range(1, 4):
-        greet({"row": (r + apart) % 4})
-    for apart in range(4):
-        greet({"gz": mate, "row": (r + apart) % 4})
-        greet({"gz": facing, "row": (r + apart) % 4})
-    greet({"gz": (g + 2) % 4})
-    for i in range(4):
-        giver = 2 * ((g % 2) * 4 + i) + g // 2
-        greet({"gz": (g + 1 + ((c - giver + 16) % 16) // 4) % 4, "col": giver})
 
     def leaf_loads(l):
         return (
@@ -203,16 +185,36 @@
         for copy in leaf_loads(l):
             copy.start()
 
+    barrier = pltpu.get_barrier_semaphore()
+
+    def greet(where):
+        pl.semaphore_signal(barrier, inc=1, device_id=where, device_id_type=MESH)
+
+    greet(sibling)
+    for apart in range(1, 8):
+        greet({"col": 2 * ((z + apart) % 8) + core})
+    for apart in range(1, 4):
+        greet({"row": (r + apart) % 4})
+    for apart in range(4):
+        greet({"gz": mate, "row": (r + apart) % 4})
+        greet({"gz": facing, "row": (r + apart) % 4})
+    greet({"gz": (g + 2) % 4})
+    for apart in (1, 7):
+        for turn in (1, 2, 3):
+            greet({"row": (r + turn) % 4, "col": 2 * ((z + apart) % 8) + core})
+    for i in range(4):
+        giver = (g % 2) * 4 + i
+        dz = (z - giver + 8) % 8
+        passed = (dz + 6) // 7 + (dz + 4) // 7 + (dz + 1) // 7
+        greet({"gz": (g + 6 - passed) % 4, "col": 2 * giver + g // 2})
+
+    holder = core * 2 + z // 4
+    turned = (g - holder + 4) % 4
+    layers_off = turned - 2 * (turned // 3)
+
     @pl.loop(0, N_LEAF)
     def _(l):
         lower_load(l).start()
-
-    @pl.loop(0, N_LEAF)
-    def _(l):
-        coupling_load(l).start()
-
-    for copy in misc:
-        copy.start()
 
     @pl.loop(0, N_LEAF)
     def _(l):
@@ -236,41 +238,40 @@
         rnd_v[:, slab(l)] = solved.astype(BF16)
         leaf_out(l).start()
 
-    pl.semaphore_wait(barrier, 24)
+    pl.semaphore_wait(barrier, 26 + 6 - 2 * layers_off)
 
     pid_copy = send(pid_v, pidsib_v, pid_sem.at[0], pid_sem.at[1], sibling)
     pid_copy.start()
 
-    def y1_copies(l):
-        return (
-            send(
-                yopp_v.at[l, pl.ds(0, y_half)], y1_v.at[l, 0], y1_ss.at[l, 0], y1_rs.at[l, 0],
-                {"row": ahead},
-            ),
-            send(
-                yopp_v.at[l, pl.ds(y_half, y_half)], y1_v.at[l, 1], y1_ss.at[l, 1],
-                y1_rs.at[l, 1], {"row": behind},
-            ),
-        )
-
-    def y2_copies(l):
-        return (
-            send(ysend_v.at[l, 0], y2_v.at[l, 0], y2_ss.at[l, 0], y2_rs.at[l, 0], {"row": ahead}),
-            send(ysend_v.at[l, 1], y2_v.at[l, 1], y2_ss.at[l, 1], y2_rs.at[l, 1], {"row": behind}),
-        )
+    def y_copy(l, apart):
+        return send(
+            y_s.at[l, (r + apart) % 4], y_r.at[l, apart - 1], y_ss.at[l], y_rs.at[l],
+            {"row": (r + apart) % 4},
+        )
+
+    def y_all(l):
+        return send(y_r.at[l], y_r.at[l], y_ss.at[l], y_rs.at[l], sibling)
 
     def sib_copy(l):
         return send(part_v.at[l], sib_v.at[l], sib_ss.at[l], sib_rs.at[l], sibling)
-
-    def to_mid(l, target):
-        return dot_nt(rnd_v[:ROWS_Y, slab(l)], lm_v[slab(target), slab(l)])
 
     @pl.loop(0, N_LEAF)
     def _(l):
         lower_load(l).wait()
-        yopp_v[l] = to_mid(l, across).astype(BF16)
-        for copy in y1_copies(l):
-            copy.start()
+        terms = dot_nt(rnd_v[:ROWS_Y, slab(l)], lm_v[:, slab(l)])
+        for i in range(4):
+            term = terms[:, i * SLICE : (i + 1) * SLICE]
+            y_s[l, i] = term.astype(BF16)
+            y_own[l, i] = term
+        for apart in (2, 1, 3):
+            y_copy(l, apart).start()
+
+    @pl.loop(0, N_LEAF)
+    def _(l):
+        coupling_load(l).start()
+
+    for copy in misc:
+        copy.start()
 
     def pairs_copy(t):
         return send(pairs_s.at[t], pairs_r.at[t], pairs_ss.at[t], pairs_rs.at[t], sibling)
@@ -297,109 +298,94 @@
 
     def z_copy(buffers, way, dist, h):
         out, into, send_sem, recv_sem = buffers
-        at = (way, dist - 1, h)
+        at = (way, dist - 2, pl.ds(*pieces[h]))
         step = 1 if way == 0 else 7
         return send(
-            out.at[at], into.at[at], send_sem.at[at], recv_sem.at[at],
+            out.at[at], into.at[at], send_sem.at[way, dist - 2, h],
+            recv_sem.at[way, dist - 2, h],
             {"col": 2 * ((z + step) % 8) + core},
         )
 
     zsum = (zsum_s, zsum_r, zsum_ss, zsum_rs)
-    flows = [
-        (way, dist, way if late else 1 - way)
-        for dist in (4, 3, 2, 1)
-        for late in (0, 1)
-        for way in (0, 1)
-        if late or dist < 4
-    ]
+    pieces = []
+    for size in PIECES:
+        pieces.append((sum(p[1] for p in pieces), size))
+
+    def flow(dist, late):
+        return [
+            (way, dist, h)
+            for i in (0, 1)
+            for way in (0, 1)
+            for h in (2 * way + i if late else 2 - 2 * way + i,)
+        ]
 
     def z_step(buffers, term_of, group):
         for way, dist, h in group:
             target = (z + dist) % 8 if way == 0 else (z + 8 - dist) % 8
             term = term_of(target, h)
-            if (way, dist + 1, h) in flows:
+            part = pl.ds(*pieces[h])
+            if dist < 3 or (dist == 3 and h // 2 == way):
                 z_copy(buffers, way, dist + 1, h).wait_recv()
-                term = term + buffers[1][way, dist, h].astype(F32)
-            buffers[0][way, dist - 1, h] = term.astype(BF16)
+                term = term + buffers[1][way, dist - 1, part].astype(F32)
+            buffers[0][way, dist - 2, part] = term.astype(BF16)
             z_copy(buffers, way, dist, h).start()
 
     def z_term(target, h):
-        part = pl.ds(h * z_half, z_half)
+        part = pl.ds(*pieces[h])
         return wide_v[target, part] + pairs_r[target, part].astype(F32)
 
     def ready(t):
         pairs_copy(t % 8).wait_recv()
 
     ready(z + 4)
-    z_step(zsum, z_term, flows[0:2])
+    z_step(zsum, z_term, flow(4, True))
     ready(z + 3)
     ready(z + 5)
-    z_step(zsum, z_term, flows[2:4])
-
-    @pl.loop(0, N_LEAF)
-    def _(l):
-        forward, backward = y1_copies(l)
-        to_ahead, to_behind = y2_copies(l)
-        term = to_mid(l, ahead)
-        forward.wait_recv()
-        ysend_v[l, 0, :y_half] = (term[:y_half] + y1_v[l, 0].astype(F32)).astype(BF16)
-        ysend_v[l, 0, y_half:] = term[y_half:].astype(BF16)
-        to_ahead.start()
-        term = to_mid(l, behind)
-        backward.wait_recv()
-        ysend_v[l, 1, :y_half] = term[:y_half].astype(BF16)
-        ysend_v[l, 1, y_half:] = (term[y_half:] + y1_v[l, 1].astype(F32)).astype(BF16)
-        to_behind.start()
+    z_step(zsum, z_term, flow(3, False))
 
     pairs(3, 8)
-    z_step(zsum, z_term, flows[4:6])
-
-    @pl.loop(0, N_LEAF)
-    def _(l):
-        coupling_load(l).wait()
-
-    for k in range(3):
-        terms = rnd_v[...].reshape(16, 16, 1024) * weight_v[k][None]
-        up_v[k] = dot_nt(terms.reshape(256, 1024), lc_v[k])
-
-    ready(z + 2)
-    ready(z + 6)
-    z_step(zsum, z_term, flows[6:8])
+    z_step(zsum, z_term, flow(3, True))
 
     acc_v[...] = jnp.zeros_like(acc_v)
 
-    def gather_parents(pids, terms):
+    def gather_parents(*groups):
         for t in range(8):
             wanted = (2 * t + core).astype(F32)
-            hit = jnp.maximum(1.0 - jnp.abs(pids - wanted), 0.0)
-            acc_v[t] += (terms.reshape(ROWS_Y // 8, 8, 128) * hit[None]).reshape(ROWS_Y, 128)
+            total = acc_v[t].reshape(ROWS_Y // 8, 8, 128)
+            for pids, terms in groups:
+                hit = jnp.maximum(1.0 - jnp.abs(pids - wanted), 0.0)
+                total = total + terms.reshape(ROWS_Y // 8, 8, 128) * hit[None]
+            acc_v[t] = total.reshape(ROWS_Y, 128)
 
     def collect(first, last):
         @pl.loop(first, last)
         def _(l):
-            term = to_mid(l, r)
-            for copy in y2_copies(l):
-                copy.wait_recv()
-            total = term + y2_v[l, 0].astype(F32) + y2_v[l, 1].astype(F32)
+            y_all(l).wait_recv()
+            total = y_own[l, r]
+            for i in range(3):
+                total = total + y_r[l, i].astype(F32)
             part_v[l] = total.astype(BF16)
             sib_copy(l).start()
-            gather_parents(pid_v[l], total)
+
+            @pl.when(l == 0)
+            def _():
+                gather_parents((pid_v[l], total))
 
             @pl.when(l > 0)
             def _():
                 sib_copy(l - 1).wait_recv()
-                gather_parents(pidsib_v[l - 1], sib_v[l - 1].astype(F32))
+                gather_parents(
+                    (pid_v[l], total), (pidsib_v[l - 1], sib_v[l - 1].astype(F32))
+                )
 
     pid_copy.wait_recv()
-    collect(0, 3)
-    z_step(zsum, z_term, flows[8:10])
-    collect(3, 6)
-    ready(z + 1)
-    ready(z + 7)
-    z_step(zsum, z_term, flows[10:12])
-    collect(6, N_LEAF)
+    collect(0, 4)
+    ready(z + 2)
+    ready(z + 6)
+    z_step(zsum, z_term, flow(2, False))
+    collect(4, N_LEAF)
     sib_copy(N_LEAF - 1).wait_recv()
-    gather_parents(pidsib_v[N_LEAF - 1], sib_v[N_LEAF - 1].astype(F32))
+    gather_parents((pidsib_v[N_LEAF - 1], sib_v[N_LEAF - 1].astype(F32)))
 
     def yz_copy(apart):
         target = (z + apart) % 8
@@ -413,26 +399,59 @@
         target = (z + apart) % 8
         yz_s[target] = acc_v[target].astype(BF16)
         yz_copy(apart).start()
-    z_step(zsum, z_term, flows[12:14])
-
-    def rs_copy(apart):
+    z_step(zsum, z_term, flow(2, True))
+
+    def own_copy(apart):
         return send(
-            rs_s.at[(r + apart) % 4], rs_r.at[apart - 1], rs_ss.at[apart - 1],
-            rs_rs.at[apart - 1], {"row": (r + apart) % 4},
-        )
+            rs_s.at[(r + apart) % 4], rs_r.at[apart - 1], rs_sem.at[0], rs_sem.at[1],
+            {"row": (r + apart) % 4},
+        )
+
+    rs_all = send(rs_r, rs_r, rs_sem.at[0], rs_sem.at[1], sibling)
+
+    def last_copy(way, h, apart):
+        target = (z + (1 if way == 0 else 7)) % 8
+        return send(
+            last_s.at[way, (r + apart) % 4, pl.ds(*pieces[h])],
+            last_r.at[way, apart, pl.ds(*pieces[h])], last_ss.at[way, h], last_rs.at[way, h],
+            {"row": (r + apart) % 4, "col": 2 * target + core},
+        )
+
+    def last_all(way, h):
+        buffer = last_r.at[way, :, pl.ds(*pieces[h])]
+        return send(buffer, buffer, last_ss.at[way, h], last_rs.at[way, h], sibling)
+
+    def last_hop(group):
+        for way, dist, h in group:
+            term = z_term((z + 1) % 8 if way == 0 else (z + 7) % 8, h)
+            z_copy(zsum, way, 2, h).wait_recv()
+            part = pl.ds(*pieces[h])
+            term = term + zsum_r[way, 0, part].astype(F32)
+            for i in range(4):
+                last_s[way, i, part] = term[:, i * SLICE : (i + 1) * SLICE].astype(BF16)
+            for apart in (2, 1, 3, 0):
+                last_copy(way, h, apart).start()
 
     ready(z)
-    for h in (0, 1):
-        for way in (0, 1):
-            z_copy(zsum, way, 1, h).wait_recv()
-        total = z_term(z, h) + zsum_r[0, 0, h].astype(F32) + zsum_r[1, 0, h].astype(F32)
-        wide_v[z, h * z_half : (h + 1) * z_half] = total
+    for h in range(4):
+        total = z_term(z, h)
+        wide_v[z, pl.ds(*pieces[h])] = total
         for i in range(4):
-            rs_s[i, h * z_half : (h + 1) * z_half] = total[:, i * SLICE : (i + 1) * SLICE].astype(
-                BF16
-            )
+            rs_s[i, pl.ds(*pieces[h])] = total[:, i * SLICE : (i + 1) * SLICE].astype(BF16)
     for apart in (2, 1, 3):
-        rs_copy(apart).start()
+        own_copy(apart).start()
+    ready(z + 1)
+    ready(z + 7)
+    last_hop(flow(1, False))
+    last_hop(flow(1, True))
+
+    @pl.loop(0, N_LEAF)
+    def _(l):
+        coupling_load(l).wait()
+
+    for k in range(3):
+        terms = rnd_v[...].reshape(16, 16, 1024) * weight_v[k][None]
+        up_v[k] = dot_nt(terms.reshape(256, 1024), lc_v[k])
 
     parts = ((0, ROWS_Y), (ROWS_Y, ROWS_Z))
 
@@ -457,12 +476,17 @@
     mt_v[r, :ROWS_Y] = total.astype(BF16)
     for apart in (2, 1, 3):
         mt_copy(0, apart).start()
-    for apart in (1, 2, 3):
-        rs_copy(apart).wait_recv()
+    rs_all.wait_recv()
     total = midrhs_v[ROWS_Y:] - wide_v[z, :, slab(r)]
     for i in range(3):
         total = total - rs_r[i].astype(F32)
-    mt_v[r, ROWS_Y:] = total.astype(BF16)
+    for h, (start, size) in enumerate(pieces):
+        part = total[start : start + size]
+        for way in (0, 1):
+            last_all(way, h).wait_recv()
+            for i in range(4):
+                part = part - last_r[way, i, start : start + size].astype(F32)
+        mt_v[r, ROWS_Y + start : ROWS_Y + start + size] = part.astype(BF16)
     for apart in (2, 1, 3):
         mt_copy(1, apart).start()
 
@@ -475,7 +499,10 @@
     misc[2].wait()
     for h in (0, 1):
         for apart in (1, 2, 3):
-            mt_arrival(h, apart).wait_recv()
+            if ROWS_Y < HALF and h == 0:
+                mt_arrival(1, apart).wait_recv()
+            if ROWS_Y >= HALF or h == 0:
+                mt_arrival(h, apart).wait_recv()
         here = slice(h * HALF, (h + 1) * HALF)
         right = jnp.concatenate([mt_v[i, here] for i in range(4)], axis=1)
         solved = dot_nt(right, pinv_v[...])
@@ -530,7 +557,7 @@
 
     @pl.loop(0, N_LEAF)
     def _(l):
-        for copy in y1_copies(l) + y2_copies(l) + (sib_copy(l), pairs_copy(l)):
+        for copy in (y_all(l), sib_copy(l), pairs_copy(l)):
             copy.wait_send()
         leaf_out(l).wait()
 
@@ -539,9 +566,15 @@
     to_rows(rsend_v, rrecv_v, 0)
     for i in range(3, 11):
         misc[i].wait()
-    for way, dist, h in flows:
+    for way, dist, h in flow(4, True) + [
+        at for dist in (3, 2) for late in (False, True) for at in flow(dist, late)
+    ]:
         z_copy(zsum, way, dist, h).wait_send()
+    for h in range(4):
+        for way in (0, 1):
+            last_all(way, h).wait_send()
     yz_all.wait_send()
+    rs_all.wait_send()
     all_of(rrecv_v, 0).wait_recv()
     for i in range(3):
         own = own + rrecv_v[i].astype(F32)
@@ -601,8 +634,6 @@
     for p in (0, 1):
         for apart in (1, 2, 3):
             mt_copy(p, apart).wait_send()
-    for apart in (1, 2, 3):
-        rs_copy(apart).wait_send()
     all_of(rrecv_v, 0).wait_send()
     all_of(q1r_v, 1).wait_send()
     all_of(er_v.at[0], 2).wait_send()
@@ -618,13 +649,20 @@
         last = last - ur_v[i].astype(F32)
     fins_v[2] = dot_nt(last.astype(BF16), apexinv_v[1])
 
-    holder = core * 2 + z // 4
-    turn = (g - holder + 7) % 4
-    for i in range(4):
-        send(
+    def final_copy(apart, other):
+        return send(
             fins_v, fin_v.at[:, rows((z % 4) * SHARE, SHARE, SHARE)], x_ss.at[6], x_rs.at[6],
-            {"gz": holder, "col": (c + 4 * turn + i) % 16},
-        ).start()
+            {"gz": holder, "col": 2 * ((z + apart) % 8) + (1 - core if other else core)},
+        )
+
+    final_reach = ((4, 3, 5), (2, 1), (0,), (6, 7))
+    for turn, reach in enumerate(final_reach):
+
+        @pl.when(turned == turn)
+        def _():
+            for apart in reach:
+                for other in (0, 1):
+                    final_copy(apart, other).start()
 
     send(tops_eight, tops_other, x_ss.at[8], x_rs.at[8], sibling).wait_recv()
     top_out = pltpu.make_async_copy(tops_v, top_o.at[0], out_misc.at[1])
@@ -635,7 +673,15 @@
     all_of(er_v.at[1], 7).wait_send()
     mid_out.wait()
     top_out.wait()
-    all_of(fin_v, 6).wait()
+    for turn, reach in enumerate(final_reach):
+
+        @pl.when(turned == turn)
+        def _():
+            for apart in reach:
+                for other in (0, 1):
+                    final_copy(apart, other).wait_send()
+
+    all_of(fin_v, 6).wait_recv()
     apex_out = pltpu.make_async_copy(fin_v, apex_o, out_misc.at[2])
     apex_out.start()
     apex_out.wait()
@@ -681,10 +727,9 @@
         V((3, 16, 1024), BF16),
         V((16, 1024), F32),
         V((3, 256, 512), F32),
-        V((8, ROWS_Y, 128), BF16),
-        V((8, 2, ROWS_Y // 2, 128), BF16),
-        V((8, 2, ROWS_Y, 128), BF16),
-        V((8, 2, ROWS_Y, 128), BF16),
+        V((8, 4, ROWS_Y, 128), BF16),
+        V((8, 4, ROWS_Y, 128), F32),
+        V((8, 3, ROWS_Y, 128), BF16),
         V((8, ROWS_Y, 128), BF16),
         V((8, ROWS_Y, 128), BF16),
         V((8, 8, 128), F32),
@@ -695,10 +740,12 @@
         V((8, ROWS_Z, 512), BF16),
         V((8, ROWS_Z, 512), BF16),
         V((8, ROWS_Z, 512), F32),
-        V((2, 4, 2, ROWS_Z // 2, 512), BF16),
-        V((2, 4, 2, ROWS_Z // 2, 512), BF16),
+        V((2, 3, ROWS_Z, 512), BF16),
+        V((2, 3, ROWS_Z, 512), BF16),
         V((4, ROWS_Z, 128), BF16),
         V((3, ROWS_Z, 128), BF16),
+        V((2, 4, ROWS_Z, 128), BF16),
+        V((2, 4, ROWS_Z, 128), BF16),
         V((4, 256, 128), BF16),
         V((256, 128), F32),
         V((3, 128, 512), BF16),
@@ -723,20 +770,19 @@
         D((11,)),
         D((8,)),
         D((3,)),
-        D((8, 2)),
-        D((8, 2)),
-        D((8, 2)),
-        D((8, 2)),
+        D((8,)),
+        D((8,)),
         D((8,)),
         D((8,)),
         D((2,)),
         D((8,)),
         D((8,)),
         D((2,)),
-        D((2, 4, 2)),
-        D((2, 4, 2)),
-        D((3,)),
-        D((3,)),
+        D((2, 3, 4)),
+        D((2, 3, 4)),
+        D((2,)),
+        D((2, 4)),
+        D((2, 4)),
         D((2, 3)),
         D((2, 3)),
         D((3,)),

time: 78.7 us -> 71.5 us (0.909)
  Pallas kernels: 77.6 us -> 70.7 us
    pallas_call x1, Pallas kernels: 75.1 us -> 68.3 us  [per_device(): pl.pallas_call(kernel, out_shape=(jax.ShapeDtypeStruct((8, 256, 128), F32...]
where the time goes in v3:
time: 71.5 us; the launch traced here: 71.4 us
  Pallas kernels  70.7 us (99%)
    pallas_call x1, Pallas kernels, per_device(): pl.pallas_call(kernel, out_shape=(jax.ShapeDtypeStruct((8, 256, 128), F32...  68.3 us
    pallas_call x1, Pallas kernels, per_device(): pl.pallas_call(place, out_shape=[jax.ShapeDtypeStruct(x.shape, x.dtype) f...  2.48 us

profile of v3, /device:TPU:1, one launch (start us, length us, event | category | flops | bytes accessed | tf_op | source)
XLA Modules:
  0.0 71.4 jit_solution(1361588501117610814)
XLA Ops:
  0.6 68.3 %tree_solve.1 = (f32[8,256,128]{2,1,0:T(8,128)}, f32[1,256,128]{2,1,0:T(8,128)}, f32[1,256,128]{2,1,0:T(8,128)}, f32[3,64,128]{2,1,0:T(8,128)}) custom-call(s32[8]{0:T(128)} %parent_s.1, s32[3,8]{1,0:T(4,128)} %bitcast.1, s32[1,2]{1,0:T(1,128)} %midpat_s.1, f32[8,256,512]{2,1,0:T(8,128)} %rhs_h.1, bf16[8,128,512]{2,1,0:T(8,128)(2,1)} %inv_h.1, ...), custom_call_target="tpu_custom_call" | custom-call | tf_op jit(solution)/shard_map/tree_solve/pallas_call | solution.py:795
  68.9 2.5 %place.1 = (f32[8,256,128]{2,1,0:T(8,128)}, f32[1,256,128]{2,1,0:T(8,128)}, f32[1,256,128]{2,1,0:T(8,128)}, f32[3,64,128]{2,1,0:T(8,128)}) custom-call(f32[8,256,128]{2,1,0:T(8,128)} %get-tuple-element.8.leaf_i, f32[1,256,128]{2,1,0:T(8,128)} %get-tuple-element.9.mid_i, f32[1,256,128]{2,1,0:T(8,128)} %get-tuple-element.10.top_i, ...), custom_call_target="tpu_custom_call" | custom-call | tf_op jit(solution)/shard_map/place/pallas_call | solution.py:815

commit v4 on v3

--- a/solution.py
+++ b/solution.py
@@ -255,23 +255,16 @@
     def sib_copy(l):
         return send(part_v.at[l], sib_v.at[l], sib_ss.at[l], sib_rs.at[l], sibling)
 
-    @pl.loop(0, N_LEAF)
-    def _(l):
-        lower_load(l).wait()
-        terms = dot_nt(rnd_v[:ROWS_Y, slab(l)], lm_v[:, slab(l)])
-        for i in range(4):
-            term = terms[:, i * SLICE : (i + 1) * SLICE]
-            y_s[l, i] = term.astype(BF16)
-            y_own[l, i] = term
-        for apart in (2, 1, 3):
-            y_copy(l, apart).start()
-
-    @pl.loop(0, N_LEAF)
-    def _(l):
-        coupling_load(l).start()
-
-    for copy in misc:
-        copy.start()
+    def products(first, last):
+        @pl.loop(first, last)
+        def _(l):
+            terms = dot_nt(rnd_v[:ROWS_Y, slab(l)], lm_v[:, slab(l)])
+            for i in range(4):
+                term = terms[:, i * SLICE : (i + 1) * SLICE]
+                y_s[l, i] = term.astype(BF16)
+                y_own[l, i] = term
+            for apart in (2, 1, 3):
+                y_copy(l, apart).start()
 
     def pairs_copy(t):
         return send(pairs_s.at[t], pairs_r.at[t], pairs_ss.at[t], pairs_rs.at[t], sibling)
@@ -293,8 +286,6 @@
             pairs_s[t] = sums[:ROWS_Z].astype(BF16)
             pairs_copy(t).start()
             wide_v[t] = sums[ROWS_Z:]
-
-    pairs(0, 3)
 
     def z_copy(buffers, way, dist, h):
         out, into, send_sem, recv_sem = buffers
@@ -337,14 +328,29 @@
     def ready(t):
         pairs_copy(t % 8).wait_recv()
 
+    @pl.loop(0, N_LEAF)
+    def _(l):
+        lower_load(l).wait()
+
+    pairs(0, 3)
+    products(0, 2)
     ready(z + 4)
     z_step(zsum, z_term, flow(4, True))
     ready(z + 3)
     ready(z + 5)
     z_step(zsum, z_term, flow(3, False))
 
+    products(2, N_LEAF)
     pairs(3, 8)
     z_step(zsum, z_term, flow(3, True))
+
+    @pl.loop(0, N_LEAF)
+    def _(l):
+        coupling_load(l).start()
+
+    for copy in misc:
+        copy.start()
+
 
     acc_v[...] = jnp.zeros_like(acc_v)
 
@@ -687,14 +693,19 @@
     apex_out.wait()
 
 
-def place(leaf_i, mid_i, top_i, apex_i, leaf_o, mid_o, top_o, apex_o, sems):
-    pairs = [(leaf_i.at[l], leaf_o.at[l]) for l in range(N_LEAF)]
-    pairs += [(mid_i, mid_o), (top_i, top_o), (apex_i, apex_o)]
-    copies = [pltpu.make_async_copy(s, d, sems.at[i]) for i, (s, d) in enumerate(pairs)]
-    for copy in copies:
-        copy.start()
-    for copy in copies:
-        copy.wait()
+def place(leaf_i, mid_i, top_i, apex_i, leaf_o, mid_o, top_o, apex_o, *scratch):
+    leaf_v, mid_v, top_v, apex_v, sems = scratch
+    parts = [(leaf_i.at[l], leaf_v.at[l], leaf_o.at[l]) for l in range(N_LEAF)]
+    parts += [(mid_i, mid_v, mid_o), (top_i, top_v, top_o), (apex_i, apex_v, apex_o)]
+    loads = [pltpu.make_async_copy(s, v, sems.at[0, i]) for i, (s, v, _) in enumerate(parts)]
+    stores = [pltpu.make_async_copy(v, d, sems.at[1, i]) for i, (_, v, d) in enumerate(parts)]
+    for load in loads:
+        load.start()
+    for load, store in zip(loads, stores):
+        load.wait()
+        store.start()
+    for store in stores:
+        store.wait()
 
 
 def per_device(*args):
@@ -789,8 +800,8 @@
         D((3,)),
         D((3,)),
         D((3,)),
-        D((9,)),
-        D((9,)),
+        D((10,)),
+        D((10,)),
     ]
     solved = pl.pallas_call(
         kernel,
@@ -815,9 +826,9 @@
     return pl.pallas_call(
         place,
         out_shape=[jax.ShapeDtypeStruct(x.shape, x.dtype) for x in solved],
-        in_specs=[pl.BlockSpec(memory_space=V)] * 4,
+        in_specs=[anywhere] * 4,
         out_specs=[anywhere] * 4,
-        scratch_shapes=[D((11,))],
+        scratch_shapes=[V(x.shape, x.dtype) for x in solved] + [D((2, 11))],
         compiler_params=pltpu.CompilerParams(vmem_limit_bytes=56 * 1024 * 1024),
         name="place",
     )(*solved)

time: 71.5 us -> 71.2 us (level)
  no operation moved by 1% of the time
where the time goes in v4:
time: 71.2 us; the launch traced here: 71 us
  Pallas kernels  70.4 us (99%)
    pallas_call x1, Pallas kernels, per_device(): pl.pallas_call(kernel, out_shape=(jax.ShapeDtypeStruct((8, 256, 128), F32...  68.1 us
    pallas_call x1, Pallas kernels, per_device(): pl.pallas_call(place, out_shape=[jax.ShapeDtypeStruct(x.shape, x.dtype) f...  2.26 us

profile of v4, /device:TPU:1, one launch (start us, length us, event | category | flops | bytes accessed | tf_op | source)
XLA Modules:
  0.0 71.0 jit_solution(3157950744082759364)
XLA Ops:
  0.6 68.1 %tree_solve.1 = (f32[8,256,128]{2,1,0:T(8,128)}, f32[1,256,128]{2,1,0:T(8,128)}, f32[1,256,128]{2,1,0:T(8,128)}, f32[3,64,128]{2,1,0:T(8,128)}) custom-call(s32[8]{0:T(128)} %parent_s.1, s32[3,8]{1,0:T(4,128)} %bitcast.1, s32[1,2]{1,0:T(1,128)} %midpat_s.1, f32[8,256,512]{2,1,0:T(8,128)} %rhs_h.1, bf16[8,128,512]{2,1,0:T(8,128)(2,1)} %inv_h.1, ...), custom_call_target="tpu_custom_call" | custom-call | tf_op jit(solution)/shard_map/tree_solve/pallas_call | solution.py:806
  68.8 2.3 %place.1 = (f32[8,256,128]{2,1,0:T(8,128)}, f32[1,256,128]{2,1,0:T(8,128)}, f32[1,256,128]{2,1,0:T(8,128)}, f32[3,64,128]{2,1,0:T(8,128)}) custom-call(f32[8,256,128]{2,1,0:T(8,128)} %get-tuple-element.8.leaf_i, f32[1,256,128]{2,1,0:T(8,128)} %get-tuple-element.9.mid_i, f32[1,256,128]{2,1,0:T(8,128)} %get-tuple-element.10.top_i, ...), custom_call_target="tpu_custom_call" | custom-call | tf_op jit(solution)/shard_map/place/pallas_call | solution.py:826
